TPU v7x, 256 devices: a whole 4x4x8 slice. The times are simulated.
256 devices in a mesh: group: 8 (over y, core), tensor: 32 (over z, x).
Axes of the slice: x: 4, y: 4, z: 8, core: 2. Of those that a mesh axis runs over, the one named last changes fastest.
Arguments:
- inputs: bfloat16 [3, 2048, 8192], P(None, ('group', 'tensor')), may hold values from -500 to 500
- norm_gain: bfloat16 [8192], replicated, may hold values from 0.099609375 to 1.8984375
- united_weight: bfloat16 [8192, 10240], P(None, 'tensor'), may hold values from -0.0625 to 0.0625
- adapter_down: bfloat16 [192, 8192, 128], P('group', 'tensor'), may hold values from -0.0625 to 0.0625
- query_up: bfloat16 [192, 64, 8192], P('group', None, 'tensor'), may hold values from -0.75 to 0.75
- value_up: bfloat16 [192, 64, 1024], P('group', None, 'tensor'), may hold values from -0.75 to 0.75
- history: bfloat16 [2048, 256, 2048], P(('group', 'tensor')), may hold values from -256 to 256
- adapter_slot: int32 [192], replicated, may hold values from 0 to 191, as said below
- row_adapter: int32 [2048], P('group'), may hold values from 0 to 191, as said below
- cache_length: int32 [2048], P('group'), may hold values from 2 to 256, as said below
Outputs:
- context: bfloat16 [3, 2048, 8192], P(None, ('group', 'tensor'))
Inputs may be any that keep to these rules, and one draw needn't show every extreme that they name: `adapter_slot`: each adapter has its own slot; slot s lies in group s // 24. `row_adapter`: row r belongs to group r // 256; all rows of one adapter lie in one group. For each ordered pair of groups, the rows of the first use at most 2 distinct adapters whose slots lie in the second, and some pair reaches 2. `cache_length`: some row reaches 256.
All inputs are finite; a program needn't handle non-finite values.
Results may differ from a plain program's by a relative error of at most 0.012.
The roundings to bfloat16 on the way count: a program that leaves them out, or rounds other values in their place, can miss the bound.
Values may be sent and summed in bfloat16 or wider, within the bound.
A program may use at most 192 MiB of HBM per device.

v0:
```python
import jax
import jax.numpy as jnp
from jax import lax
from jax.sharding import PartitionSpec as P

HEADS = 64
KV_HEADS = 8
HEAD_DIM = 128
PAIR_MOST = 2


adapter_scale = 0.5
rope_base = 500000.0
norm_eps = 1e-05


def batched_product(pattern, first_operand, second_operand):
    return jnp.einsum(pattern, first_operand, second_operand, preferred_element_type=jnp.float32)


def rms_normed(inputs, norm_gain):
    values = inputs.astype(jnp.float32)
    mean_square = jnp.mean(values * values, axis=-1, keepdims=True)
    return (values * lax.rsqrt(mean_square + norm_eps) * norm_gain.astype(jnp.float32)).astype(
        jnp.bfloat16
    )


def rotate(heads_in, positions):
    head_width = heads_in.shape[-1]
    halfway = head_width // 2
    ladder = jnp.arange(halfway).astype(jnp.float32) * (2.0 / head_width)
    inverse = jnp.power(jnp.float32(rope_base), -ladder)
    angles = positions.astype(jnp.float32)[..., None, None] * inverse
    cosine = jnp.cos(angles)
    sine_part = jnp.sin(angles)
    values = heads_in.astype(jnp.float32)
    leading = values[..., :halfway]
    trailing = values[..., halfway:]
    turned = jnp.concatenate(
        [leading * cosine - trailing * sine_part, trailing * cosine + leading * sine_part], axis=-1
    )
    return turned.astype(jnp.bfloat16)


def attend(queries, new_keys, new_values, history, lengths, current):
    row_count, head_count, head_width = queries.shape
    kv_count = new_keys.shape[2]
    kv_width = kv_count * head_width
    window = history.shape[1]
    past_keys = history[:, :, :kv_width].reshape(row_count, window, kv_count, head_width)
    past_values = history[:, :, kv_width:].reshape(row_count, window, kv_count, head_width)
    grouped = queries.reshape(row_count, kv_count, head_count // kv_count, head_width)
    factor = head_width ** (-0.5)
    past_scores = batched_product("rkgd,rpkd->rkgp", grouped, past_keys) * factor
    fresh_scores = batched_product("rkgd,jrkd->rkgj", grouped, new_keys) * factor
    past_live = jnp.arange(window)[None, :] < lengths[:, None]
    fresh_live = jnp.arange(new_keys.shape[0]) <= current
    past_scores = jnp.where(past_live[:, None, None, :], past_scores, -jnp.inf)
    fresh_scores = jnp.where(fresh_live, fresh_scores, -jnp.inf)
    highest = jnp.maximum(jnp.max(past_scores, axis=-1), jnp.max(fresh_scores, axis=-1))[..., None]
    past_exp = jnp.exp(past_scores - highest)
    fresh_exp = jnp.exp(fresh_scores - highest)
    denominator = jnp.sum(past_exp, axis=-1, keepdims=True) + jnp.sum(
        fresh_exp, axis=-1, keepdims=True
    )
    past_weights = (past_exp / denominator).astype(jnp.bfloat16)
    fresh_weights = (fresh_exp / denominator).astype(jnp.bfloat16)
    context = batched_product("rkgp,rpkd->rkgd", past_weights, past_values) + batched_product(
        "rkgj,jrkd->rkgd", fresh_weights, new_values
    )
    return context.reshape(row_count, head_count * head_width).astype(jnp.bfloat16)


def local(
    inputs,
    norm_gain,
    united_weight,
    adapter_down,
    query_up,
    value_up,
    history,
    adapter_slot,
    row_adapter,
    cache_length,
):
    sections, rows_here, model_width = inputs.shape
    shards = lax.axis_size("tensor")
    groups = lax.axis_size("group")
    own_index = lax.axis_index("tensor")
    home_group = lax.axis_index("group")
    block_span_width = united_weight.shape[1]
    query_portion = model_width // shards
    key_portion = (block_span_width - query_portion) // 2
    rank_size = query_up.shape[1]
    store_size = adapter_down.shape[0]
    slots_all = adapter_slot.shape[0]
    normed = rms_normed(inputs, norm_gain)
    catalog = jnp.arange(slots_all, dtype=jnp.int32)
    by_adapter = row_adapter[:, None] == catalog[None, :]
    slot_of_row = jnp.sum(jnp.where(by_adapter, adapter_slot[None, :], 0), axis=1)
    by_slot = slot_of_row[:, None] == catalog[None, :]
    source = slot_of_row // store_size
    offset = slot_of_row % store_size
    wanted = jnp.any(by_slot, axis=0).reshape(groups, store_size)
    foreign = jnp.logical_and(wanted, jnp.arange(groups, dtype=jnp.int32)[:, None] != home_group)
    marked = foreign.astype(jnp.int32)
    ranking = jnp.cumsum(marked, axis=1) - marked
    chosen = jnp.logical_and(
        foreign[:, :, None],
        ranking[:, :, None] == jnp.arange(PAIR_MOST, dtype=jnp.int32)[None, None, :],
    )
    request = jnp.sum(
        jnp.where(chosen, jnp.arange(store_size, dtype=jnp.int32)[None, :, None], 0), axis=1
    )
    asked_for = lax.all_to_all(request, "group", split_axis=0, concat_axis=0, tiled=True)
    outgoing = (
        jnp.take(adapter_down, asked_for, axis=0),
        jnp.take(query_up, asked_for, axis=0),
        jnp.take(value_up, asked_for, axis=0),
    )
    incoming = (
        lax.all_to_all(outgoing[0], "group", split_axis=0, concat_axis=0, tiled=True),
        lax.all_to_all(outgoing[1], "group", split_axis=0, concat_axis=0, tiled=True),
        lax.all_to_all(outgoing[2], "group", split_axis=0, concat_axis=0, tiled=True),
    )
    extra_down = incoming[0].reshape((-1,) + adapter_down.shape[1:])
    extra_query = incoming[1].reshape((-1,) + query_up.shape[1:])
    extra_value = incoming[2].reshape((-1,) + value_up.shape[1:])
    down_table = jnp.concatenate([adapter_down, extra_down], axis=0)
    query_table = jnp.concatenate([query_up, extra_query], axis=0)
    value_table = jnp.concatenate([value_up, extra_value], axis=0)
    row_rank = jnp.sum(jnp.where(by_slot, ranking.reshape(-1)[None, :], 0), axis=1)
    table_row = jnp.where(source == home_group, offset, store_size + source * PAIR_MOST + row_rank)
    entries = down_table.shape[0]
    selector = table_row[:, None] == jnp.arange(entries, dtype=jnp.int32)[None, :]
    query_flat = query_table.reshape(entries * rank_size, query_table.shape[2])
    value_flat = value_table.reshape(entries * rank_size, value_table.shape[2])
    own_lengths = lax.dynamic_slice_in_dim(cache_length, own_index * rows_here, rows_here, 0)
    key_list = []
    value_list = []
    results = []
    for step_index in range(sections):
        gathered_rows = lax.all_gather(
            normed[step_index : step_index + 1], "tensor", axis=1, tiled=True
        )
        own_inputs = lax.dynamic_slice_in_dim(
            gathered_rows, own_index * query_portion, query_portion, 2
        )
        base_part = batched_product("snd,dc->snc", gathered_rows, united_weight)
        every_entry = batched_product("nd,edk->nek", own_inputs[0], down_table)
        shrink_list = [jnp.sum(jnp.where(selector[:, :, None], every_entry, 0.0), axis=1)]
        combined_heads = jnp.concatenate([base_part, jnp.stack(shrink_list)], axis=2)
        summed = lax.psum(combined_heads[:, :, block_span_width:], "tensor")
        lowrank = summed.astype(jnp.bfloat16)
        count_now = lowrank.shape[0]
        group_rows = lowrank.shape[1]
        zero_low = jnp.zeros((), jnp.bfloat16)
        spread_query = jnp.where(
            selector[None, :, :, None], lowrank[:, :, None, :rank_size], zero_low
        ).reshape(count_now, group_rows, entries * rank_size)
        spread_value = jnp.where(
            selector[None, :, :, None], lowrank[:, :, None, rank_size:], zero_low
        ).reshape(count_now, group_rows, entries * rank_size)
        updated_query = combined_heads[:, :, :query_portion] + adapter_scale * batched_product(
            "snk,kc->snc", spread_query, query_flat
        )
        key_new = combined_heads[:, :, query_portion : query_portion + key_portion]
        updated_value = combined_heads[
            :, :, query_portion + key_portion : block_span_width
        ] + adapter_scale * batched_product("snk,kc->snc", spread_value, value_flat)
        fresh_rows = jnp.concatenate([updated_query, key_new, updated_value], axis=2).astype(
            jnp.bfloat16
        )
        spread = lax.all_to_all(fresh_rows, "tensor", split_axis=1, concat_axis=2, tiled=True)
        arranged = spread.reshape(count_now, rows_here, shards, block_span_width)
        query_all = arranged[:, :, :, :query_portion].reshape(count_now, rows_here, HEADS, HEAD_DIM)
        key_all = arranged[:, :, :, query_portion : query_portion + key_portion].reshape(
            count_now, rows_here, KV_HEADS, HEAD_DIM
        )
        value_all = arranged[:, :, :, query_portion + key_portion :].reshape(
            count_now, rows_here, KV_HEADS, HEAD_DIM
        )
        positions = (
            own_lengths[None, :] + (step_index + jnp.arange(count_now, dtype=jnp.int32))[:, None]
        )
        query_rot = rotate(query_all, positions)
        key_rot = rotate(key_all, positions)
        key_list.append(key_rot[0])
        value_list.append(value_all[0])
        results.append(
            attend(
                query_rot[0],
                jnp.stack(key_list),
                jnp.stack(value_list),
                history,
                own_lengths,
                step_index,
            )
        )
    return jnp.stack(results)


def solution(mesh):
    in_specs = (
        P(None, ("group", "tensor"), None),
        P(),
        P(None, "tensor"),
        P("group", "tensor", None),
        P("group", None, "tensor"),
        P("group", None, "tensor"),
        P(("group", "tensor"), None, None),
        P(),
        P("group"),
        P("group"),
    )
    out_specs = P(None, ("group", "tensor"), None)
    return jax.shard_map(local, mesh=mesh, in_specs=in_specs, out_specs=out_specs, check_vma=False)
```

profile of v0, /device:TPU:8, one launch (start us, length us, event | category | flops | bytes accessed | tf_op | source)
XLA Modules:
  0.0 496.1 jit_solution(4920474618669396588)
XLA Ops:
  6.5 1.2 fusion.131
  8.5 1.2 fusion.133
  11.9 0.8 select_reduce_fusion.4
  14.0 5.3 %all-to-all-start = ((s32[8,1,2]{2,1,0:T(1,128)}), s32[8,1,2]{2,1,0:T(1,128)S(1)}, u32[]{:S(2)}, u32[]{:S(2)}) async-start(s32[8,1,2]{2,1,0:T(1,128)} %copy.122), calls=%async_computation | async-start | bytes 8192 | tf_op jit(solution)/shard_map/all_to_all | solution.py:116
  19.6 6.1 %fusion.236 = (bf16[8,256,1024]{2,1,0:T(8,128)(2,1)}, bf16[8,256,1024]{2,1,0:T(8,128)(2,1)}) fusion(bf16[8,256,2048]{2,1,0:T(8,128)(2,1)} %param.16), kind=kLoop, calls=%fused_computation.277 | loop fusion | bytes 16777216 | tf_op jit(solution)/shard_map/slice | solution.py:51
  25.6 6.4 %copy.174 = bf16[8,256,1024]{1,2,0:T(8,128)(2,1)} copy(bf16[8,256,1024]{2,1,0:T(8,128)(2,1)} %get-tuple-element.12) | data formatting | bytes 8388608
  32.1 6.6 %copy.175 = bf16[8,256,1024]{1,2,0:T(8,128)(2,1)} copy(bf16[8,256,1024]{2,1,0:T(8,128)(2,1)} %get-tuple-element.13) | data formatting | bytes 8388608
  40.8 4.8 all-to-all-start.3
  46.4 1.1 broadcast_select_fusion
  47.5 2.3 all-to-all-done.3
  49.8 4.9 all-to-all-start.1
  54.9 1.7 gather_fusion.1
  56.6 0.9 broadcast_select_fusion.1
  57.5 0.8 reshape.1014
  58.3 10.9 %all-to-all-done.1 = bf16[8,2,256,128]{3,2,1,0:T(8,128)(2,1)S(1)} async-done(((bf16[8,2,256,128]{3,2,1,0:T(8,128)(2,1)}), bf16[8,2,256,128]{3,2,1,0:T(8,128)(2,1)S(1)}, u32[]{:S(2)}, u32[]{:S(2)}) %all-to-all-start.1) | async-done | bytes 1048608 | tf_op jit(solution)/shard_map/all_to_all | solution.py:123
  69.3 4.8 all-to-all-start.2
  74.1 21.0 %all-gather.6.cloned.1.call-done = bf16[1,256,8192]{2,1,0:T(8,128)(2,1)} async-done(((bf16[1,8,8192]{2,1,0:T(8,128)(2,1)}), bf16[1,256,8192]{2,1,0:T(8,128)(2,1)}) %all-gather.6.cloned.1.call-update) | async-done | bytes 4194320 | tf_op jit(solution)/shard_map/all_gather | solution.py:144
  95.2 3.8 select_reduce_fusion.1
  99.0 77.9 %all-gather.8.cloned.1.call-done = bf16[1,256,8192]{2,1,0:T(8,128)(2,1)} async-done(((bf16[1,8,8192]{2,1,0:T(8,128)(2,1)}), bf16[1,256,8192]{2,1,0:T(8,128)(2,1)}) %all-gather.8.cloned.1.call-update) | async-done | bytes 4194320 | tf_op jit(solution)/shard_map/all_gather | solution.py:144
  176.9 4.6 select_reduce_fusion
  181.6 4.9 fusion.30
  186.5 2.3 fusion.33
  188.8 69.9 %all-gather.4.cloned.1.call-done = bf16[1,256,8192]{2,1,0:T(8,128)(2,1)} async-done(((bf16[1,8,8192]{2,1,0:T(8,128)(2,1)}), bf16[1,256,8192]{2,1,0:T(8,128)(2,1)}) %all-gather.4.cloned.1.call-update) | async-done | bytes 4194320 | tf_op jit(solution)/shard_map/all_gather | solution.py:144
  258.7 5.3 %fusion.27 = f32[1,256,320]{1,2,0:T(8,128)S(1)} fusion(bf16[8192,320]{0,1:T(8,128)(2,1)} %param.12, bf16[1,256,8192]{2,1,0:T(8,128)(2,1)} %all-gather.4.cloned.1.call-done), kind=kOutput, calls=%fused_computation.38 | convolution fusion | flops 1342177280 | bytes 9764864 | tf_op jit(solution)/shard_map/snd,dc->snc/dot_general | solution.py:18
  264.1 4.6 select_reduce_fusion.2
  268.7 0.9 slice.287
  270.3 143.9 %all-reduce.2 = (bf16[1,256,128]{2,1,0:T(8,128)(2,1)S(1)}, bf16[1,256,128]{2,1,0:T(8,128)(2,1)S(1)}, bf16[1,256,128]{2,1,0:T(8,128)(2,1)S(1)}) all-reduce(f32[1,256,128]{2,1,0:T(8,128)} %bitcast.266, f32[1,256,128]{2,1,0:T(8,128)S(1)} %bitcast.265, f32[1,256,128]{2,1,0:T(8,128)} %bitcast.267), channel_id=1, replica_groups=mesh['group'=8,'tensor'=32] {'tensor'}, use_global_device_ids=true, to_apply=%region_17.18 | all-reduce | flops 98304 | bytes 589824 | tf_op jit(solution)/shard_map/psum | solution.py:154
  414.7 1.9 fusion.75
  420.2 1.9 reduce.2
  422.0 0.9 reshape.1019
  423.4 1.9 reduce.1
  425.3 0.9 reshape.1017
  426.2 5.4 %all-to-all-start.5 = ((bf16[32,2,1280]{2,1,0:T(2,128)(2,1)}), bf16[32,2,1280]{2,1,0:T(2,128)(2,1)S(1)}, u32[]{:S(2)}, u32[]{:S(2)}) async-start(bf16[32,2,1280]{2,1,0:T(2,128)(2,1)} %reshape.1017), calls=%async_computation.5 | async-start | bytes 327680 | tf_op jit(solution)/shard_map/all_to_all | solution.py:175
  431.7 1.1 fusion.128
  433.3 1.9 reduce
  435.2 0.9 reshape.1015
  436.1 6.3 %all-to-all-done.5 = bf16[32,2,1280]{2,1,0:T(2,128)(2,1)S(1)} async-done(((bf16[32,2,1280]{2,1,0:T(2,128)(2,1)}), bf16[32,2,1280]{2,1,0:T(2,128)(2,1)S(1)}, u32[]{:S(2)}, u32[]{:S(2)}) %all-to-all-start.5) | async-done | bytes 163872 | tf_op jit(solution)/shard_map/all_to_all | solution.py:175
  442.4 3.9 all-to-all-start.6
  446.8 10.4 %all-to-all-done.6 = bf16[32,2,1280]{2,1,0:T(2,128)(2,1)S(1)} async-done(((bf16[32,2,1280]{2,1,0:T(2,128)(2,1)}), bf16[32,2,1280]{2,1,0:T(2,128)(2,1)S(1)}, u32[]{:S(2)}, u32[]{:S(2)}) %all-to-all-start.6) | async-done | bytes 163872 | tf_op jit(solution)/shard_map/all_to_all | solution.py:175
  457.1 4.1 all-to-all-start.4
  461.7 10.1 %all-to-all-done.4 = bf16[32,2,1280]{2,1,0:T(2,128)(2,1)S(1)} async-done(((bf16[32,2,1280]{2,1,0:T(2,128)(2,1)}), bf16[32,2,1280]{2,1,0:T(2,128)(2,1)S(1)}, u32[]{:S(2)}, u32[]{:S(2)}) %all-to-all-start.4) | async-done | bytes 163872 | tf_op jit(solution)/shard_map/all_to_all | solution.py:175
  475.0 3.3 fusion.244
  478.3 0.8 fusion.240
  479.1 0.8 fusion.242
  482.3 1.2 fusion.73
  483.5 1.2 fusion.149
  485.2 3.4 fusion.72
  488.8 0.8 pad_maximum_fusion.5
  (153 shorter events, 19.7 us)
Async XLA Ops:
  6.5 88.6 %all-gather.6.cloned.1.call-start = ((), (), s32[]{:S(2)}) async-start(), calls=%async_computation.8 | async-start | bytes 4325376 | tf_op jit(solution)/shard_map/all_gather | solution.py:144
  10.4 166.6 %all-gather.8.cloned.1.call-start = ((), (), s32[]{:S(2)}) async-start(), calls=%async_computation.9 | async-start | bytes 4325376 | tf_op jit(solution)/shard_map/all_gather | solution.py:144
  11.1 247.6 %all-gather.4.cloned.1.call-start = ((), (), s32[]{:S(2)}) async-start(), calls=%async_computation.7 | async-start | bytes 4325376 | tf_op jit(solution)/shard_map/all_gather | solution.py:144
  14.0 25.0 %all-to-all-start = ((s32[8,1,2]{2,1,0:T(1,128)}), s32[8,1,2]{2,1,0:T(1,128)S(1)}, u32[]{:S(2)}, u32[]{:S(2)}) async-start(s32[8,1,2]{2,1,0:T(1,128)} %copy.122), calls=%async_computation | async-start | bytes 8192 | tf_op jit(solution)/shard_map/all_to_all | solution.py:116
  32.1 6.6 %copy-start.9 = (s32[256]{0:T(256)S(1)}, s32[256]{0:T(256)}, u32[]{:S(2)}) copy-start(s32[256]{0:T(256)} %param.19) | copy-start | bytes 3076
  32.1 7.3 %copy-start.4 = (bf16[24,64,32]{1,2,0:T(8,128)(2,1)S(1)}, bf16[24,64,32]{1,2,0:T(8,128)(2,1)}, u32[]{:S(2)}) copy-start(bf16[24,64,32]{1,2,0:T(8,128)(2,1)} %param.15) | copy-start | bytes 294916
  32.1 13.6 %copy-start.2 = (bf16[24,256,128]{2,1,0:T(8,128)(2,1)S(1)}, bf16[24,256,128]{2,1,0:T(8,128)(2,1)}, u32[]{:S(2)}) copy-start(bf16[24,256,128]{2,1,0:T(8,128)(2,1)} %param.13) | copy-start | bytes 4718596
  40.8 9.0 %all-to-all-start.3 = ((bf16[8,2,2048]{2,1,0:T(2,128)(2,1)}), bf16[8,2,2048]{2,1,0:T(2,128)(2,1)S(1)}, u32[]{:S(2)}, u32[]{:S(2)}) async-start(bf16[8,2,2048]{2,1,0:T(2,128)(2,1)} %reshape.1013), calls=%async_computation.3 | async-start | bytes 131072 | tf_op jit(solution)/shard_map/all_to_all | solution.py:125
  49.8 19.5 %all-to-all-start.1 = ((bf16[8,2,256,128]{3,2,1,0:T(8,128)(2,1)}), bf16[8,2,256,128]{3,2,1,0:T(8,128)(2,1)S(1)}, u32[]{:S(2)}, u32[]{:S(2)}) async-start(bf16[8,2,256,128]{3,2,1,0:T(8,128)(2,1)} %broadcast_select_fusion), calls=%async_computation.1 | async-start | bytes 2097152 | tf_op jit(solution)/shard_map/all_to_all | solution.py:123
  69.3 345.4 %all-to-all-start.2 = ((bf16[8,2,64,256]{3,2,1,0:T(8,128)(2,1)}), bf16[8,2,64,256]{3,2,1,0:T(8,128)(2,1)S(1)}, u32[]{:S(2)}, u32[]{:S(2)}) async-start(bf16[8,2,64,256]{3,2,1,0:T(8,128)(2,1)} %broadcast_select_fusion.1), calls=%async_computation.2 | async-start | bytes 1048576 | tf_op jit(solution)/shard_map/all_to_all | solution.py:124
  176.9 4.6 copy-start.10
  176.9 9.6 %slice-start = ((s8[5242880]{0:T(1024)(128)(4,1)}), s8[4194304]{0:T(1024)(128)(4,1)S(1)}, s32[]{:S(2)}) async-start(s8[5242880]{0:T(1024)(128)(4,1)} %bitcast.274), calls=%async_computation.10 | async-start | bytes 8388608
  181.6 4.9 slice-start.1
  181.6 4.9 copy-start.11
  264.0 6.2 %copy-start.7 = (f32[1,256,320]{1,2,0:T(8,128)}, f32[1,256,320]{1,2,0:T(8,128)S(1)}, u32[]{:S(2)}) copy-start(f32[1,256,320]{1,2,0:T(8,128)S(1)} %fusion.27) | copy-start | bytes 983044
  268.6 148.0 %copy-start.3 = (bf16[24,64,256]{2,1,0:T(8,128)(2,1)S(1)}, bf16[24,64,256]{2,1,0:T(8,128)(2,1)}, u32[]{:S(2)}) copy-start(bf16[24,64,256]{2,1,0:T(8,128)(2,1)} %param.14) | copy-start | bytes 2359300
  268.7 148.0 %copy-start.6 = (f32[1,256,320]{1,2,0:T(8,128)S(1)}, f32[1,256,320]{1,2,0:T(8,128)}, u32[]{:S(2)}) copy-start(f32[1,256,320]{1,2,0:T(8,128)} %fusion.30) | copy-start | bytes 983044
  414.7 2.8 copy-start.8
  416.7 1.7 copy-start.5
  426.2 16.2 %all-to-all-start.5 = ((bf16[32,2,1280]{2,1,0:T(2,128)(2,1)}), bf16[32,2,1280]{2,1,0:T(2,128)(2,1)S(1)}, u32[]{:S(2)}, u32[]{:S(2)}) async-start(bf16[32,2,1280]{2,1,0:T(2,128)(2,1)} %reshape.1017), calls=%async_computation.5 | async-start | bytes 327680 | tf_op jit(solution)/shard_map/all_to_all | solution.py:175
  442.4 14.7 %all-to-all-start.6 = ((bf16[32,2,1280]{2,1,0:T(2,128)(2,1)}), bf16[32,2,1280]{2,1,0:T(2,128)(2,1)S(1)}, u32[]{:S(2)}, u32[]{:S(2)}) async-start(bf16[32,2,1280]{2,1,0:T(2,128)(2,1)} %reshape.1015), calls=%async_computation.6 | async-start | bytes 327680 | tf_op jit(solution)/shard_map/all_to_all | solution.py:175
  457.1 14.7 %all-to-all-start.4 = ((bf16[32,2,1280]{2,1,0:T(2,128)(2,1)}), bf16[32,2,1280]{2,1,0:T(2,128)(2,1)S(1)}, u32[]{:S(2)}, u32[]{:S(2)}) async-start(bf16[32,2,1280]{2,1,0:T(2,128)(2,1)} %reshape.1019), calls=%async_computation.4 | async-start | bytes 327680 | tf_op jit(solution)/shard_map/all_to_all | solution.py:175
  474.3 4.0 copy-start
  479.9 2.4 copy-start.1
Sparse Core Ops, SparseCore 0:
  10.5 84.6 all-gather.5
  97.8 79.1 all-gather.7
  179.5 79.1 all-gather.3
where the time goes:
time: 497 us; the launch traced here: 496 us
  waiting for transfers between devices  210 us (42%)
  blocking collectives  144 us (29%)
  matrix products  43.4 us (9%)
  local copies, waits for them, and re-layouts  35.3 us (7%)
  starting transfers between devices  33.4 us (7%)
  other arithmetic  15.8 us (3%)
  between operations  13.9 us (3%)
    all_gather x3, waiting for transfers between devices, local(): lax.all_gather(normed[step_index:step_index + 1], 'tensor', axis=1, tiled...  169 us
    psum x1, blocking collectives, local(): summed = lax.psum(combined_heads[:, :, block_span_width:], 'tensor')  144 us
    dot_general x23, matrix products, batched_product(): jnp.einsum(pattern, first_operand, second_operand, preferred_element_type...  43.4 us
    all_to_all x3, waiting for transfers between devices, local(): lax.all_to_all(fresh_rows, 'tensor', split_axis=1, concat_axis=2, tiled=T...  26.9 us
    unnamed x43, local copies, waits for them, and re-layouts  19 us
    all_to_all x3, starting transfers between devices, local(): lax.all_to_all(fresh_rows, 'tensor', split_axis=1, concat_axis=2, tiled=T...  13.4 us
    all_to_all x1, waiting for transfers between devices, local(): lax.all_to_all(outgoing[0], 'group', split_axis=0, concat_axis=0, tiled=T...  10.9 us
  transfers between devices with their start and end apart: 10, of which 8 were waited for; matrix products, arithmetic and copies ran while one was open for 12% of the time, Pallas kernels for 0%

commit v1 on v0

v1 whole, which is shorter than its diff:
```python
import functools

import jax
import jax.numpy as jnp
from jax import lax
from jax.experimental import pallas as pl
from jax.experimental.pallas import tpu as pltpu
from jax.sharding import PartitionSpec as P

HEADS = 64
KV_HEADS = 8
HEAD_DIM = 128
PAIR_MOST = 2
NX = 4

adapter_scale = 0.5
rope_base = 500000.0
norm_eps = 1e-05
MIB = 1024 * 1024
F32 = jnp.float32
BF16 = jnp.bfloat16
MESH = pl.DeviceIdType.MESH


def rms_normed(inputs, norm_gain):
    values = inputs.astype(F32)
    mean_square = jnp.mean(values * values, axis=-1, keepdims=True)
    return (values * lax.rsqrt(mean_square + norm_eps) * norm_gain.astype(F32)).astype(BF16)


def rotate(heads_in, positions):
    head_width = heads_in.shape[-1]
    halfway = head_width // 2
    ladder = jnp.arange(halfway).astype(F32) * (2.0 / head_width)
    inverse = jnp.power(F32(rope_base), -ladder)
    angles = positions.astype(F32)[..., None, None] * inverse
    cosine = jnp.cos(angles)
    sine_part = jnp.sin(angles)
    values = heads_in.astype(F32)
    leading = values[..., :halfway]
    trailing = values[..., halfway:]
    turned = jnp.concatenate(
        [leading * cosine - trailing * sine_part, trailing * cosine + leading * sine_part], axis=-1
    )
    return turned.astype(BF16)


def project_kernel(
    nx, nz, ng, own,
    xk, xl, w, down, qup, vup, req, tr,
    out,
    X, wv, lbuf, xs, down_o, q_o, v_o, down_f, q_f, v_f, sd, sq, sv, rbuf, rs,
    part, pbuf, S, sbuf, lrz, lrall, LRq, LRv, Dq, Dv, acc, ob,
    ssem, gsem, lsem, dsem, fsem, qsem, p1, p2, p3, p4, osem, wsem,
):
    nt = nx * nz
    K2 = X.shape[1]
    NW = w.shape[1]
    rank = 64
    tiles = K2 // 128
    ta = max((tiles * 13) // 32, 2)
    LA = ta * 128
    LB = K2 - LA
    spans = {
        "A": ((0, (ta // 2) * 128), ((ta // 2) * 128, LA - (ta // 2) * 128)),
        "B": ((LA, ((tiles - ta) // 2) * 128), (LA + ((tiles - ta) // 2) * 128, LB - ((tiles - ta) // 2) * 128)),
    }
    whole = {"A": (0, LA), "B": (LA, LB)}
    which = {"A": 0, "B": 1}

    g = lax.axis_index("group")
    t = lax.axis_index("tensor")
    z = t // nx
    x = t % nx

    def dev(dx, dz):
        return lax.rem(z + (dz % nz), nz) * nx + lax.rem(x + (dx % nx), nx)

    pending = []
    counter = [0]

    def remote(src, dst, rsem, group, tensor):
        sem = ssem.at[counter[0]]
        counter[0] += 1
        copy = pltpu.make_async_remote_copy(
            src_ref=src, dst_ref=dst, send_sem=sem, recv_sem=rsem,
            device_id=(group, tensor), device_id_type=MESH,
        )
        copy.start()
        pending.append(copy)

    def arrived(ref, sem):
        pltpu.make_async_copy(ref, ref, sem).wait()

    barrier = pltpu.get_barrier_semaphore()

    def greet(k, carry):
        pl.semaphore_signal(barrier, inc=1, device_id=(g, lax.rem(t + k, nt)), device_id_type=MESH)
        return carry

    lax.fori_loop(1, nt, greet, 0)

    def greet_group(k, carry):
        pl.semaphore_signal(barrier, inc=1, device_id=(lax.rem(g + k, ng), t), device_id_type=MESH)
        return carry

    lax.fori_loop(1, ng, greet_group, 0)

    mine = pl.multiple_of(t * 48, 16)
    loads = [
        pltpu.make_async_copy(xk, X.at[pl.ds(mine, 48), :], wsem.at[0]),
        pltpu.make_async_copy(down, down_o, wsem.at[1]),
        pltpu.make_async_copy(qup, q_o, wsem.at[2]),
        pltpu.make_async_copy(vup, v_o, wsem.at[3]),
        pltpu.make_async_copy(w.at[pl.ds(0, K2), :], wv.at[0], wsem.at[4]),
        pltpu.make_async_copy(w.at[pl.ds(K2, K2), :], wv.at[1], wsem.at[5]),
        pltpu.make_async_copy(xl.at[pl.ds(mine, 48), :], lbuf.at[pl.ds(mine, 48), :], wsem.at[6]),
    ]
    for load in loads:
        load.start()
    loads[0].wait()

    pl.semaphore_wait(barrier, nt - 1 + ng - 1)

    def piece(dx, dz, lo, n):
        rows = pl.multiple_of(dev(dx, dz) * 48, 16)
        return X.at[pl.ds(rows, 48), pl.ds(lo, n)]

    def forward(name, dx, dz, half, axis, step):
        lo, n = whole[name] if half is None else spans[name][half]
        ref = piece(dx, dz, lo, n)
        if axis == "x":
            there = dev(step, 0)
            ndx, ndz = (dx - step) % nx, dz % nz
        else:
            there = dev(0, step)
            ndx, ndz = dx % nx, (dz - step) % nz
        remote(ref, ref, gsem.at[which[name], ndx, ndz, 0 if half is None else half], g, there)

    def expect(name, dx, dz, half):
        lo, n = whole[name] if half is None else spans[name][half]
        arrived(piece(dx, dz, lo, n), gsem.at[which[name], dx % nx, dz % nz, 0 if half is None else half])

    def launch(name, dx, dz, axis):
        size = nx if axis == "x" else nz
        if size // 2 > 1:
            forward(name, dx, dz, None, axis, 1)
            forward(name, dx, dz, None, axis, -1)
        elif size == 2:
            forward(name, dx, dz, 0, axis, 1)
            forward(name, dx, dz, 1, axis, -1)

    def relay(name, dx, dz, axis, k, sign):
        size = nx if axis == "x" else nz
        if k + 1 < size // 2:
            forward(name, dx, dz, None, axis, -sign)
        elif k + 1 == size // 2:
            forward(name, dx, dz, 0 if sign < 0 else 1, axis, -sign)

    def wave(name, axis, k, other):
        size = nx if axis == "x" else nz
        if k < size // 2:
            for sign in (-1, 1):
                dx, dz = (sign * k, other) if axis == "x" else (other, sign * k)
                expect(name, dx, dz, None)
                relay(name, dx, dz, axis, k, sign)
        elif size > 1:
            dx, dz = (k, other) if axis == "x" else (other, k)
            expect(name, dx, dz, 0)
            expect(name, dx, dz, 1)

    for k in range(1, nt):
        peer = lax.rem(t + k, nt)
        remote(
            xl.at[pl.ds(pl.multiple_of(peer * 48, 16), 48), :],
            lbuf.at[pl.ds(mine, 48), :], lsem.at[nt - k], g, peer,
        )
    for k in range(1, ng):
        peer = lax.rem(g + k, ng)
        remote(req.at[peer], rbuf.at[g], qsem.at[ng - k], peer, t)

    launch("A", 0, 0, "x")
    launch("B", 0, 0, "z")
    launch("B", 0, 0, "x")
    launch("A", 0, 0, "z")

    for load in loads[1:4]:
        load.wait()
    down_f[pl.ds(g * 2, 2)] = jnp.zeros((2,) + down_f.shape[1:], BF16)
    q_f[pl.ds(pl.multiple_of(g * 2 * rank, 16), 2 * rank), :] = jnp.zeros((2 * rank, q_f.shape[1]), BF16)
    v_f[pl.ds(pl.multiple_of(g * 2 * rank, 16), 2 * rank), :] = jnp.zeros((2 * rank, v_f.shape[1]), BF16)
    for k in range(1, ng):
        peer = lax.rem(g + k, ng)
        arrived(rbuf.at[peer], qsem.at[k])
        down_copy = pltpu.make_async_copy(rbuf.at[peer], rs.at[k], wsem.at[7])
        down_copy.start()
        down_copy.wait()
        for j in range(PAIR_MOST):
            slot = rs[k, 0, j]
            sd[k, j] = down_o[slot]
            sq[k, j] = q_o[slot]
            sv[k, j] = v_o[slot]
        here = pl.multiple_of(g * 2 * rank, 16)
        remote(sd.at[k], down_f.at[pl.ds(g * 2, 2)], fsem.at[ng - k, 0], peer, t)
        for j in range(PAIR_MOST):
            spot = pl.ds(pl.multiple_of((g * 2 + j) * rank, 16), rank)
            remote(sq.at[k, j], q_f.at[spot, :], fsem.at[ng - k, 1 + j], peer, t)
            remote(sv.at[k, j], v_f.at[spot, :], fsem.at[ng - k, 3 + j], peer, t)

    wave("A", "x", 1, 0)
    if nx == 4:
        launch("A", 1, 0, "z")
        launch("A", -1, 0, "z")
    wave("B", "z", 1, 0)
    for sign in ((-1, 1) if nz > 2 else (1,)):
        if nz > 1:
            launch("B", 0, sign, "x")
    if nx == 4:
        wave("A", "x", 2, 0)
        launch("A", 2, 0, "z")
    elif nx == 2:
        launch("A", 1, 0, "z")

    loads[6].wait()
    for k in range(1, nt):
        arrived(lbuf.at[pl.ds(pl.multiple_of(lax.rem(t + k, nt) * 48, 16), 48), :], lsem.at[k])
    both = lbuf[...].astype(F32).reshape(nt, 2, 24, 128)
    xs[...] = jnp.concatenate([both[:, 0], both[:, 1]], axis=-1).reshape(nt * 24, 256)

    def shrink(table, first):
        def body(e, carry):
            chosen = tr[...] == e + first
            pick = jnp.concatenate([chosen, chosen], axis=-1)
            rows = jnp.where(pick, xs[...], 0.0).astype(BF16)
            part[...] += jnp.dot(rows, table[e], preferred_element_type=F32)
            return carry
        return body

    part[...] = jnp.zeros(part.shape, F32)
    lax.fori_loop(0, own, shrink(down_o, 0), 0)

    for k in range(2, nz // 2 + 1):
        wave("B", "z", k, 0)
        for sign in ((-1, 1) if k < nz // 2 else (1,)):
            launch("B", 0, sign * k, "x")

    for k in range(1, ng):
        peer = lax.rem(g + k, ng)
        arrived(down_f.at[pl.ds(peer * 2, 2)], fsem.at[k, 0])
    lax.fori_loop(0, ng * PAIR_MOST, shrink(down_f, own), 0)

    for zz in range(nz):
        for xx in range(nx):
            S[xx, zz] = part[pl.ds((zz * nx + xx) * 24, 24), :]
    for k in range(1, nx):
        peer = lax.rem(x + k, nx)
        remote(S.at[peer], pbuf.at[x], p1.at[nx - k], g, z * nx + peer)

    def finish_x(dz):
        for k in range(1, nx // 2 + 1):
            wave("B", "x", k, dz)

    def a_wave(k):
        for dx in range(nx):
            wave("A", "z", k, dx)

    finish_x(0)

    pbuf[pl.ds(x, 1)] = S[pl.ds(x, 1)]
    for k in range(1, nx):
        arrived(pbuf.at[lax.rem(x + k, nx)], p1.at[k])
    total = pbuf[0]
    for xx in range(1, nx):
        total = total + pbuf[xx]
    pbuf[0] = total
    for k in range(1, nz):
        peer = lax.rem(z + k, nz)
        remote(pbuf.at[0, peer], sbuf.at[z], p2.at[nz - k], g, peer * nx + x)

    if nz > 1:
        a_wave(1)

    sbuf[pl.ds(z, 1)] = pbuf[0, pl.ds(z, 1)]
    for k in range(1, nz):
        arrived(sbuf.at[lax.rem(z + k, nz)], p2.at[k])
    low = sbuf[0]
    for zz in range(1, nz):
        low = low + sbuf[zz]
    low = jnp.concatenate([low, jnp.zeros((8, 128), F32)], axis=0).astype(BF16)
    lrz[pl.ds(z, 1)] = low[None]
    for k in range(1, nz):
        peer = lax.rem(z + k, nz)
        remote(lrz.at[z], lrz.at[z], p3.at[nz - k], g, peer * nx + x)

    for load in loads[4:6]:
        load.wait()

    kt = 512

    def base_of(dz):
        rows = pl.ds(pl.multiple_of(lax.rem(z + dz % nz, nz) * (nx * 48), 16), nx * 48)
        acc[...] = jnp.zeros(acc.shape, F32)

        def body(k, carry):
            cols = pl.ds(pl.multiple_of(k * kt, kt), kt)
            for h in range(2):
                acc[h] += jnp.dot(X[rows, cols], wv[h, cols, :], preferred_element_type=F32)
            return carry

        lax.fori_loop(0, K2 // kt, body, 0)
        first = acc[0].reshape(nx * 3, 2, 8, NW)[:, 0]
        second = acc[1].reshape(nx * 3, 2, 8, NW)[:, 1]
        return (first + second).reshape(nx * 24, NW)

    def finish(dz):
        base = base_of(dz)
        zz = lax.rem(z + dz % nz, nz)
        rows = pl.ds(pl.multiple_of(zz * (nx * 24), 8), nx * 24)
        query = base[:, :256] + adapter_scale * Dq[rows, :]
        keyval = base[:, 256:320] + adapter_scale * Dv[rows, :][:, :64]
        for xx in range(nx):
            q = query[xx * 24 : xx * 24 + 24]
            kv = keyval[xx * 24 : xx * 24 + 24]
            block = jnp.concatenate(
                [
                    q[:, :128], q[:, 128:],
                    jnp.concatenate([kv[0:8], kv[8:16]], axis=-1),
                    jnp.concatenate([kv[16:24], jnp.zeros((8, 64), F32)], axis=-1),
                ],
                axis=0,
            )
            ob[dz % nz, xx] = block.astype(BF16)
        for dx in range(nx):
            xx = lax.rem(x + dx, nx)
            if dx == 0 and dz % nz == 0:
                keep = pltpu.make_async_copy(ob.at[0, xx], out.at[t], wsem.at[8])
                keep.start()
                keep.wait()
            else:
                remote(ob.at[dz % nz, xx], out.at[t], osem.at[(-dx) % nx, (-dz) % nz], g, zz * nx + xx)

    for k in range(1, nz):
        arrived(lrz.at[lax.rem(z + k, nz)], p3.at[k])
    lrall[pl.ds(x, 1)] = lrz[...][None]
    for k in range(1, nx):
        peer = lax.rem(x + k, nx)
        remote(lrz, lrall.at[x], p4.at[nx - k], g, z * nx + peer)

    for k in range(1, nx):
        arrived(lrall.at[lax.rem(x + k, nx)], p4.at[k])
    for k in range(1, ng):
        peer = lax.rem(g + k, ng)
        for j in range(PAIR_MOST):
            spot = pl.ds(pl.multiple_of((peer * 2 + j) * rank, 16), rank)
            arrived(q_f.at[spot, :], fsem.at[k, 1 + j])
            arrived(v_f.at[spot, :], fsem.at[k, 3 + j])

    for zz in range(nz):
        for xx in range(nx):
            low24 = lrall[xx, zz].astype(F32)[:24]
            spot = pl.ds((zz * nx + xx) * 24, 24)
            LRq[spot, :] = jnp.concatenate([low24[:, :64], low24[:, :64]], axis=-1)
            LRv[spot, :] = jnp.concatenate([low24[:, 64:], low24[:, 64:]], axis=-1)
    Dq[...] = jnp.zeros(Dq.shape, F32)
    Dv[...] = jnp.zeros(Dv.shape, F32)

    def grow(q_table, v_table, first):
        def body(i, carry):
            lane = lax.broadcasted_iota(jnp.int32, (nt * 24, 128), 1) // 64
            hit0 = tr[...] == lane + (i * 4 + first)
            hit1 = tr[...] == lane + (i * 4 + 2 + first)
            spread_q = jnp.concatenate([jnp.where(hit0, LRq[...], 0.0), jnp.where(hit1, LRq[...], 0.0)], axis=-1)
            spread_v = jnp.concatenate([jnp.where(hit0, LRv[...], 0.0), jnp.where(hit1, LRv[...], 0.0)], axis=-1)
            Dq[...] += jnp.dot(spread_q.astype(BF16), q_table(i), preferred_element_type=F32)
            Dv[...] += jnp.dot(spread_v.astype(BF16), v_table(i), preferred_element_type=F32)
            return carry
        return body

    def own_table(ref):
        return lambda i: ref[pl.ds(i * 4, 4)].reshape(4 * rank, ref.shape[2])

    def far_table(ref):
        return lambda i: ref[pl.ds(pl.multiple_of(i * 4 * rank, 4 * rank), 4 * rank), :]

    lax.fori_loop(0, own // 4, grow(own_table(q_o), own_table(v_o), 0), 0)
    lax.fori_loop(0, ng * PAIR_MOST // 4, grow(far_table(q_f), far_table(v_f), own), 0)

    finish(0)
    for k in range(1, nz // 2 + 1):
        if k > 1:
            a_wave(k)
        for sign in ((-1, 1) if k < nz // 2 else (1,)):
            finish_x(sign * k)
            finish(sign * k)

    for dz in range(nz):
        for dx in range(nx):
            if dx or dz:
                arrived(out.at[dev(dx, dz)], osem.at[dx, dz])
    for copy in pending:
        copy.wait_send()


def project(nx, nz, ng, xk, xl, w, down, qup, vup, req, tr):
    nt = nx * nz
    K2 = xk.shape[1]
    own = down.shape[0]
    NW = w.shape[1]
    DMA = pltpu.SemaphoreType.DMA
    vmem = pl.BlockSpec(memory_space=pltpu.VMEM)
    hbm = pl.BlockSpec(memory_space=pl.ANY)
    sends = (nt - 1) + (ng - 1) * 6 + 5 * nt + 2 * (nx + nz) + 64 + nt + 160
    rows = nt * 24
    return pl.pallas_call(
        functools.partial(project_kernel, nx, nz, ng, own),
        out_shape=jax.ShapeDtypeStruct((nt, 64, 128), BF16),
        in_specs=[vmem, vmem, hbm, hbm, hbm, hbm, vmem, vmem],
        out_specs=vmem,
        scratch_shapes=[
            pltpu.VMEM((nt * 48, K2), BF16),
            pltpu.VMEM((2, K2, NW), BF16),
            pltpu.VMEM((nt * 48, 128), BF16),
            pltpu.VMEM((rows, 256), F32),
            pltpu.VMEM(down.shape, BF16),
            pltpu.VMEM(qup.shape, BF16),
            pltpu.VMEM(vup.shape, BF16),
            pltpu.VMEM((ng * 2,) + down.shape[1:], BF16),
            pltpu.VMEM((ng * 2 * 64, 256), BF16),
            pltpu.VMEM((ng * 2 * 64, 128), BF16),
            pltpu.VMEM((ng, 2) + down.shape[1:], BF16),
            pltpu.VMEM((ng, 2, 64, 256), BF16),
            pltpu.VMEM((ng, 2, 64, 128), BF16),
            pltpu.VMEM((ng, 8, 128), jnp.int32),
            pltpu.SMEM((ng, 8, 128), jnp.int32),
            pltpu.VMEM((rows, 128), F32),
            pltpu.VMEM((nx, nz, 24, 128), F32),
            pltpu.VMEM((nx, nz, 24, 128), F32),
            pltpu.VMEM((nz, 24, 128), F32),
            pltpu.VMEM((nz, 32, 128), BF16),
            pltpu.VMEM((nx, nz, 32, 128), BF16),
            pltpu.VMEM((rows, 128), F32),
            pltpu.VMEM((rows, 128), F32),
            pltpu.VMEM((rows, 256), F32),
            pltpu.VMEM((rows, 128), F32),
            pltpu.VMEM((2, nx * 48, NW), F32),
            pltpu.VMEM((nz, nx, 64, 128), BF16),
            DMA((sends,)),
            DMA((2, nx, nz, 2)),
            DMA((nt,)),
            DMA((1,)),
            DMA((ng, 5)),
            DMA((ng,)),
            DMA((nx,)),
            DMA((nz,)),
            DMA((nz,)),
            DMA((nx,)),
            DMA((nx, nz)),
            DMA((9,)),
        ],
        compiler_params=pltpu.CompilerParams(
            collective_id=0, has_side_effects=True, vmem_limit_bytes=56 * MIB
        ),
        name="project",
    )(xk, xl, w, down, qup, vup, req, tr)


def attend_kernel(lengths, q, fk, fv, hist, out):
    row = pl.program_id(0)
    window = hist.shape[1]
    kv_width = hist.shape[2] // 2
    length = lengths[row]
    factor = HEAD_DIM ** (-0.5)
    past_live = lax.broadcasted_iota(jnp.int32, (32, window), 1) < length
    step = lax.broadcasted_iota(jnp.int32, (32, 16), 0) // 8
    fresh_at = lax.broadcasted_iota(jnp.int32, (32, 16), 1)
    fresh_live = jnp.logical_and(fresh_at <= step, fresh_at < 3)
    for h in range(KV_HEADS):
        keys = hist[0, :, h * HEAD_DIM : (h + 1) * HEAD_DIM]
        values = hist[0, :, kv_width + h * HEAD_DIM : kv_width + (h + 1) * HEAD_DIM]
        queries = q[0, h]
        dims = (((1,), (1,)), ((), ()))
        past = lax.dot_general(queries, keys, dims, preferred_element_type=F32) * factor
        fresh = lax.dot_general(queries, fk[0, h], dims, preferred_element_type=F32) * factor
        past = jnp.where(past_live, past, -jnp.inf)
        fresh = jnp.where(fresh_live, fresh, -jnp.inf)
        highest = jnp.maximum(
            jnp.max(past, axis=-1, keepdims=True), jnp.max(fresh, axis=-1, keepdims=True)
        )
        past = jnp.exp(past - highest)
        fresh = jnp.exp(fresh - highest)
        total = jnp.sum(past, axis=-1, keepdims=True) + jnp.sum(fresh, axis=-1, keepdims=True)
        past = (past / total).astype(BF16)
        fresh = (fresh / total).astype(BF16)
        context = jnp.dot(past, values, preferred_element_type=F32) + jnp.dot(
            fresh, fv[0, h], preferred_element_type=F32
        )
        out[0, h] = context.astype(BF16)


def attend(lengths, q, fk, fv, hist):
    rows, window, width = hist.shape
    return pl.pallas_call(
        attend_kernel,
        out_shape=jax.ShapeDtypeStruct((rows, KV_HEADS, 32, HEAD_DIM), BF16),
        grid=(rows,),
        in_specs=[
            pl.BlockSpec(memory_space=pltpu.SMEM),
            pl.BlockSpec((1, KV_HEADS, 32, HEAD_DIM), lambda r: (r, 0, 0, 0)),
            pl.BlockSpec((1, KV_HEADS, 16, HEAD_DIM), lambda r: (r, 0, 0, 0)),
            pl.BlockSpec((1, KV_HEADS, 16, HEAD_DIM), lambda r: (r, 0, 0, 0)),
            pl.BlockSpec((1, window, width), lambda r: (r, 0, 0)),
        ],
        out_specs=pl.BlockSpec((1, KV_HEADS, 32, HEAD_DIM), lambda r: (r, 0, 0, 0)),
        compiler_params=pltpu.CompilerParams(vmem_limit_bytes=32 * MIB),
        name="attend",
    )(lengths, q, fk, fv, hist)


def routing(adapter_slot, row_adapter, store, groups, home):
    slots = adapter_slot.shape[0]
    catalog = jnp.arange(slots, dtype=jnp.int32)
    by_adapter = row_adapter[:, None] == catalog[None, :]
    slot_of_row = jnp.sum(jnp.where(by_adapter, adapter_slot[None, :], 0), axis=1)
    by_slot = slot_of_row[:, None] == catalog[None, :]
    source = slot_of_row // store
    offset = slot_of_row % store
    wanted = jnp.any(by_slot, axis=0).reshape(groups, store)
    foreign = jnp.logical_and(wanted, jnp.arange(groups, dtype=jnp.int32)[:, None] != home)
    marked = foreign.astype(jnp.int32)
    ranking = jnp.cumsum(marked, axis=1) - marked
    chosen = jnp.logical_and(
        foreign[:, :, None],
        ranking[:, :, None] == jnp.arange(PAIR_MOST, dtype=jnp.int32)[None, None, :],
    )
    request = jnp.sum(
        jnp.where(chosen, jnp.arange(store, dtype=jnp.int32)[None, :, None], 0), axis=1
    )
    row_rank = jnp.sum(jnp.where(by_slot, ranking.reshape(-1)[None, :], 0), axis=1)
    table_row = jnp.where(source == home, offset, store + source * PAIR_MOST + row_rank)
    return request, table_row


def projected(
    inputs, norm_gain, united_weight, adapter_down, query_up, value_up, adapter_slot, row_adapter
):
    steps, rows_here, width = inputs.shape
    nt = lax.axis_size("tensor")
    ng = lax.axis_size("group")
    nx = NX
    nz = nt // nx
    g = lax.axis_index("group")
    half = width // 2
    request, table_row = routing(adapter_slot, row_adapter, adapter_down.shape[0], ng, g)
    normed = rms_normed(inputs, norm_gain)
    xk = normed.reshape(steps, rows_here, 2, half).transpose(0, 2, 1, 3).reshape(steps * 2 * rows_here, half)
    xl = normed.reshape(steps * rows_here, nt * 2, 128).transpose(1, 0, 2).reshape(nt * 48, 128)
    req = jnp.pad(request[:, None, :], ((0, 0), (0, 7), (0, 128 - PAIR_MOST)))
    tr = jnp.broadcast_to(table_row.reshape(nt, 1, rows_here, 1), (nt, steps, rows_here, 128))
    tr = tr.reshape(nt * steps * rows_here, 128)
    vpad = jnp.pad(value_up, ((0, 0), (0, 0), (32, 64)))
    return project(nx, nz, ng, xk, xl, united_weight, adapter_down, query_up, vpad, req, tr)


def local(
    inputs, norm_gain, united_weight, adapter_down, query_up, value_up, history,
    adapter_slot, row_adapter, cache_length,
):
    steps, rows_here, width = inputs.shape
    nt = lax.axis_size("tensor")
    t = lax.axis_index("tensor")
    got = projected(
        inputs, norm_gain, united_weight, adapter_down, query_up, value_up, adapter_slot, row_adapter
    )
    lengths = lax.dynamic_slice_in_dim(cache_length, t * rows_here, rows_here, 0)
    query = got[:, :48].reshape(nt, 2, steps, rows_here, HEAD_DIM)
    query = query.transpose(2, 3, 0, 1, 4).reshape(steps, rows_here, HEADS, HEAD_DIM)
    fresh = got[:, 48:].reshape(nt, 2, rows_here, 2, 64).transpose(0, 2, 1, 3, 4)
    fresh = fresh.reshape(nt, rows_here, 4, 64)[:, :, :steps].transpose(2, 1, 0, 3)
    key = fresh[..., :32].reshape(steps, rows_here, KV_HEADS, HEAD_DIM)
    value = fresh[..., 32:].reshape(steps, rows_here, KV_HEADS, HEAD_DIM)
    positions = lengths[None, :] + jnp.arange(steps, dtype=jnp.int32)[:, None]
    query = rotate(query, positions)
    key = rotate(key, positions)
    q = query.reshape(steps, rows_here, KV_HEADS, HEADS // KV_HEADS, HEAD_DIM)
    q = q.transpose(1, 2, 0, 3, 4).reshape(rows_here, KV_HEADS, 24, HEAD_DIM)
    q = jnp.pad(q, ((0, 0), (0, 0), (0, 8), (0, 0)))
    fk = jnp.pad(key.transpose(1, 2, 0, 3), ((0, 0), (0, 0), (0, 13), (0, 0)))
    fv = jnp.pad(value.transpose(1, 2, 0, 3), ((0, 0), (0, 0), (0, 13), (0, 0)))
    context = attend(lengths, q, fk, fv, history)
    context = context[:, :, :24].reshape(rows_here, KV_HEADS, steps, HEADS // KV_HEADS, HEAD_DIM)
    return context.transpose(2, 0, 1, 3, 4).reshape(steps, rows_here, width)


def solution(mesh):
    in_specs = (
        P(None, ("group", "tensor"), None),
        P(),
        P(None, "tensor"),
        P("group", "tensor", None),
        P("group", None, "tensor"),
        P("group", None, "tensor"),
        P(("group", "tensor"), None, None),
        P(),
        P("group"),
        P("group"),
    )
    out_specs = P(None, ("group", "tensor"), None)
    return jax.shard_map(local, mesh=mesh, in_specs=in_specs, out_specs=out_specs, check_vma=False)
```

time: 497 us -> 229 us (0.46)
  waiting for transfers between devices: 210 us -> 0 us
  Pallas kernels: 0 us -> 200 us
  blocking collectives: 144 us -> 0 us
  matrix products: 43.4 us -> 0 us
  starting transfers between devices: 33.4 us -> 0 us
  local copies, waits for them, and re-layouts: 35.3 us -> 20.6 us
  between operations: 13.9 us -> 0.29 us
  other arithmetic: 15.8 us -> 7.72 us
    pallas_call x0 -> x2, Pallas kernels: none -> 200 us  [the longest x1 176 us: project(): pl.pallas_call(functools.partial(project_kernel, nx, nz, ng, own), out_sh...]
    all_gather x3 -> x0, waiting for transfers between devices: 169 us -> none  [local(): lax.all_gather(normed[step_index:step_index + 1], 'tensor', axis=1, tiled...]
    psum x1 -> x0, blocking collectives: 144 us -> none  [local(): summed = lax.psum(combined_heads[:, :, block_span_width:], 'tensor')]
    dot_general x23 -> x0, matrix products: 43.4 us -> none  [batched_product(): jnp.einsum(pattern, first_operand, second_operand, preferred_element_type...]
    all_to_all x7 -> x0, waiting for transfers between devices: 40.1 us -> none  [the longest x3 26.9 us: local(): lax.all_to_all(fresh_rows, 'tensor', split_axis=1, concat_axis=2, tiled=T...]
    all_to_all x7 -> x0, starting transfers between devices: 33.3 us -> none  [the longest x3 13.4 us: local(): lax.all_to_all(fresh_rows, 'tensor', split_axis=1, concat_axis=2, tiled=T...]
    unnamed x43 -> x9, local copies, waits for them, and re-layouts: 19 us -> 11.9 us
    slice x8 -> x4, local copies, waits for them, and re-layouts: 8.44 us -> 2.06 us  [the longest x1 1.03 us: local(): query = got[:, :48].reshape(nt, 2, steps, rows_here, HEAD_DIM)]
  transfers between devices with their start and end apart: 10 -> 0, of which waited for: 8 -> 0; matrix products, arithmetic and copies ran while one was open for 12% -> 0% of each run, Pallas kernels for 0% -> 0%
where the time goes in v1:
time: 229 us
  Pallas kernels  200 us (87%)
  local copies, waits for them, and re-layouts  20.6 us (9%)
  other arithmetic  7.72 us (3%)
    pallas_call x1, Pallas kernels, project(): pl.pallas_call(functools.partial(project_kernel, nx, nz, ng, own), out_sh...  176 us
    pallas_call x1, Pallas kernels, attend(): pl.pallas_call(attend_kernel, out_shape=jax.ShapeDtypeStruct((rows, KV_HE...  23.7 us
    unnamed x9, local copies, waits for them, and re-layouts  11.9 us

profile of v1, /device:TPU:8, one launch (start us, length us, event | category | flops | bytes accessed | tf_op | source)
XLA Modules:
  0.0 228.7 jit_solution(18322379665326940058)
XLA Ops:
  0.0 0.8 select_reduce_fusion.1
  0.8 0.1 fusion.5
  0.9 0.1 reshape.200
  1.0 0.1 fusion.13
  1.1 0.2 reduce_window_sum.13
  1.3 0.1 reduce_window_sum.14
  1.4 0.1 and.49
  1.4 0.1 and.55
  1.5 0.1 select_reduce_fusion
  1.7 0.1 reduce_sum.42
  1.8 0.1 div.18
  1.8 0.1 rem.24
  2.0 0.1 ne.53
  2.1 0.1 broadcast_in_dim.67
  2.2 0.9 broadcast_in_dim.68.tr
  3.1 0.1 select_reduce_fusion.2
  3.3 0.1 copy.50
  3.3 0.6 pad.20.req
  4.0 0.7 convert_element_type.67
  4.7 1.2 fusion
  5.9 1.2 fusion.16
  7.0 0.1 copy.65
  7.1 1.0 copy.48
  8.1 1.9 fusion.2
  10.1 8.2 %copy.51.w = bf16[8192,320]{1,0:T(8,128)(2,1)} copy(bf16[8192,320]{0,1:T(8,128)(2,1)} %param.12) | data formatting | bytes 10485760 | tf_op args[2]
  18.3 0.2 copy.49
  18.5 0.9 pad.19.vup
  19.4 176.5 %project.1 = bf16[32,64,128]{2,1,0:T(8,128)(2,1)} custom-call(bf16[48,4096]{1,0:T(8,128)(2,1)} %bitcast.50, bf16[1536,128]{1,0:T(8,128)(2,1)} %bitcast.49, bf16[8192,320]{1,0:T(8,128)(2,1)} %copy.51.w, bf16[24,256,128]{2,1,0:T(8,128)(2,1)} %down.1, bf16[24,64,256]{2,1,0:T(8,128)(2,1)} %qup.1, bf16[24,64,128]{2,1,0:T(8,128)(2,1)} %pad.19.vup, ...), custom_call_target="tpu_custom_call" | custom-call | tf_op jit(solution)/shard_map/project/pallas_call | solution.py:414
  195.9 0.9 slice.33
  196.8 0.1 reshape.202
  197.0 0.1 fusion.14
  197.2 0.1 copy.55
  197.3 0.1 reshape.208
  197.4 0.1 fusion.15
  197.5 0.1 dynamic_slice.3.lengths
  197.6 0.1 multiply_cosine_fusion
  197.8 0.1 fusion.7
  197.9 0.1 maximum_bitcast_fusion.1
  198.1 1.0 slice.30
  199.2 0.4 copy.52
  199.6 0.4 fusion.3
  200.0 0.2 copy_bitcast_fusion
  200.2 0.1 pad.21.q
  200.3 0.1 reshape.204
  200.6 3.4 %copy-done = bf16[8,256,2048]{2,1,0:T(8,128)(2,1)S(1)} copy-done((bf16[8,256,2048]{2,1,0:T(8,128)(2,1)S(1)}, bf16[8,256,2048]{2,1,0:T(8,128)(2,1)}, u32[]{:S(2)}) %copy-start) | copy-done | bytes 8388632
  203.9 23.7 %attend.1 = bf16[8,8,32,128]{3,2,1,0:T(8,128)(2,1)S(1)} custom-call(s32[8]{0:T(128)S(1)} %dynamic_slice.3.lengths, bf16[8,8,32,128]{3,2,1,0:T(8,128)(2,1)S(1)} %pad.21.q, bf16[8,8,16,128]{3,2,1,0:T(8,128)(2,1)S(1)} %pad.22.fk, bf16[8,8,16,128]{3,2,1,0:T(8,128)(2,1)S(1)} %pad.23.fv, bf16[8,256,2048]{2,1,0:T(8,128)(2,1)S(1)} %copy-done), custom_call_target="tpu_custom_call" | custom-call | tf_op jit(solution)/shard_map/attend/pallas_call | solution.py:502
  227.6 0.1 slice_bitcast_fusion
  227.7 1.0 copy.62
  (24 shorter events, 0.4 us)
Async XLA Ops:
  8.1 10.1 %copy-start.1 = (bf16[24,64,32]{1,2,0:T(8,128)(2,1)S(1)}, bf16[24,64,32]{1,2,0:T(8,128)(2,1)}, u32[]{:S(2)}) copy-start(bf16[24,64,32]{1,2,0:T(8,128)(2,1)} %param.15) | copy-start | bytes 294916
  19.4 178.1 %copy-start.2 = (s32[256]{0:T(256)S(1)}, s32[256]{0:T(256)}, u32[]{:S(2)}) copy-start(s32[256]{0:T(256)} %param.19) | copy-start | bytes 3076
  200.6 3.4 %copy-start = (bf16[8,256,2048]{2,1,0:T(8,128)(2,1)S(1)}, bf16[8,256,2048]{2,1,0:T(8,128)(2,1)}, u32[]{:S(2)}) copy-start(bf16[8,256,2048]{2,1,0:T(8,128)(2,1)} %hist.1) | copy-start | bytes 25165828

commit v2 on v1

--- a/solution.py
+++ b/solution.py
@@ -1,4 +1,5 @@
 import functools
+import heapq
 
 import jax
 import jax.numpy as jnp
@@ -45,20 +46,78 @@
     return turned.astype(BF16)
 
 
+CHORES = (3.0, 18.0, 50.0, 57.0, 63.0, 68.0, 73.0)
+BUSY = {"x": 4.0, "z": 8.0}
+RATE = 45e3
+
+
+def ring_order(nx, nz, la, lb):
+    sizes = {"A": la * 96 / RATE, "B": lb * 96 / RATE}
+    span = {"x": nx, "z": nz}
+    free = {(axis, step): BUSY[axis] for axis in "xz" for step in (1, -1)}
+    heap = []
+    halves = {}
+    out = []
+    count = [0]
+
+    def send(now, name, dx, dz, half, axis, step):
+        key = (axis, step)
+        start = max(free[key], now)
+        free[key] = start + sizes[name] * (1.0 if half is None else 0.5)
+        out.append(("send", key, name, dx % nx, dz % nz, half))
+        ndx = (dx - (step if axis == "x" else 0)) % nx
+        ndz = (dz - (step if axis == "z" else 0)) % nz
+        count[0] += 1
+        heapq.heappush(heap, (free[key] + 1.5, count[0], name, ndx, ndz, half, axis, step))
+
+    def launch(now, name, dx, dz, axis):
+        if span[axis] > 2:
+            send(now, name, dx, dz, None, axis, 1)
+            send(now, name, dx, dz, None, axis, -1)
+        elif span[axis] == 2:
+            send(now, name, dx, dz, 0, axis, 1)
+            send(now, name, dx, dz, 1, axis, -1)
+
+    launch(0.0, "A", 0, 0, "x")
+    launch(0.0, "B", 0, 0, "z")
+    launch(0.0, "B", 0, 0, "x")
+    launch(0.0, "A", 0, 0, "z")
+    while heap:
+        now, _, name, dx, dz, half, axis, step = heapq.heappop(heap)
+        tie = (name, dx, dz)
+        seen = halves.get(tie, 0)
+        halves[tie] = seen + 1
+        last = half is None or seen == 1
+        out.append(("wait", now, name, dx, dz, half if half is None else (half, last)))
+        size = span[axis]
+        far = (-step * (dx if axis == "x" else dz)) % size
+        if half is None:
+            if far + 1 < size // 2:
+                send(now, name, dx, dz, None, axis, step)
+            elif far + 1 == size // 2:
+                send(now, name, dx, dz, 0 if step > 0 else 1, axis, step)
+        if last:
+            if name == "A" and axis == "x":
+                launch(now, name, dx, dz, "z")
+            if name == "B" and axis == "z":
+                launch(now, name, dx, dz, "x")
+    return out
+
+
 def project_kernel(
     nx, nz, ng, own,
     xk, xl, w, down, qup, vup, req, tr,
     out,
     X, wv, lbuf, xs, down_o, q_o, v_o, down_f, q_f, v_f, sd, sq, sv, rbuf, rs,
-    part, pbuf, S, sbuf, lrz, lrall, LRq, LRv, Dq, Dv, acc, ob,
+    part, pbuf, S, sbuf, lrz, lrall, LRq, LRv, Dq, Dv, acc, plain, ob,
     ssem, gsem, lsem, dsem, fsem, qsem, p1, p2, p3, p4, osem, wsem,
 ):
     nt = nx * nz
     K2 = X.shape[1]
-    NW = w.shape[1]
+    NW = w.shape[0]
     rank = 64
     tiles = K2 // 128
-    ta = max((tiles * 13) // 32, 2)
+    ta = max((tiles * 12) // 32, 2)
     LA = ta * 128
     LB = K2 - LA
     spans = {
@@ -112,8 +171,8 @@
         pltpu.make_async_copy(down, down_o, wsem.at[1]),
         pltpu.make_async_copy(qup, q_o, wsem.at[2]),
         pltpu.make_async_copy(vup, v_o, wsem.at[3]),
-        pltpu.make_async_copy(w.at[pl.ds(0, K2), :], wv.at[0], wsem.at[4]),
-        pltpu.make_async_copy(w.at[pl.ds(K2, K2), :], wv.at[1], wsem.at[5]),
+        pltpu.make_async_copy(w.at[:, pl.ds(0, K2)], wv.at[0], wsem.at[4]),
+        pltpu.make_async_copy(w.at[:, pl.ds(K2, K2)], wv.at[1], wsem.at[5]),
         pltpu.make_async_copy(xl.at[pl.ds(mine, 48), :], lbuf.at[pl.ds(mine, 48), :], wsem.at[6]),
     ]
     for load in loads:
@@ -141,34 +200,6 @@
         lo, n = whole[name] if half is None else spans[name][half]
         arrived(piece(dx, dz, lo, n), gsem.at[which[name], dx % nx, dz % nz, 0 if half is None else half])
 
-    def launch(name, dx, dz, axis):
-        size = nx if axis == "x" else nz
-        if size // 2 > 1:
-            forward(name, dx, dz, None, axis, 1)
-            forward(name, dx, dz, None, axis, -1)
-        elif size == 2:
-            forward(name, dx, dz, 0, axis, 1)
-            forward(name, dx, dz, 1, axis, -1)
-
-    def relay(name, dx, dz, axis, k, sign):
-        size = nx if axis == "x" else nz
-        if k + 1 < size // 2:
-            forward(name, dx, dz, None, axis, -sign)
-        elif k + 1 == size // 2:
-            forward(name, dx, dz, 0 if sign < 0 else 1, axis, -sign)
-
-    def wave(name, axis, k, other):
-        size = nx if axis == "x" else nz
-        if k < size // 2:
-            for sign in (-1, 1):
-                dx, dz = (sign * k, other) if axis == "x" else (other, sign * k)
-                expect(name, dx, dz, None)
-                relay(name, dx, dz, axis, k, sign)
-        elif size > 1:
-            dx, dz = (k, other) if axis == "x" else (other, k)
-            expect(name, dx, dz, 0)
-            expect(name, dx, dz, 1)
-
     for k in range(1, nt):
         peer = lax.rem(t + k, nt)
         remote(
@@ -179,53 +210,29 @@
         peer = lax.rem(g + k, ng)
         remote(req.at[peer], rbuf.at[g], qsem.at[ng - k], peer, t)
 
-    launch("A", 0, 0, "x")
-    launch("B", 0, 0, "z")
-    launch("B", 0, 0, "x")
-    launch("A", 0, 0, "z")
-
-    for load in loads[1:4]:
-        load.wait()
-    down_f[pl.ds(g * 2, 2)] = jnp.zeros((2,) + down_f.shape[1:], BF16)
-    q_f[pl.ds(pl.multiple_of(g * 2 * rank, 16), 2 * rank), :] = jnp.zeros((2 * rank, q_f.shape[1]), BF16)
-    v_f[pl.ds(pl.multiple_of(g * 2 * rank, 16), 2 * rank), :] = jnp.zeros((2 * rank, v_f.shape[1]), BF16)
-    for k in range(1, ng):
-        peer = lax.rem(g + k, ng)
-        arrived(rbuf.at[peer], qsem.at[k])
-        down_copy = pltpu.make_async_copy(rbuf.at[peer], rs.at[k], wsem.at[7])
-        down_copy.start()
-        down_copy.wait()
-        for j in range(PAIR_MOST):
-            slot = rs[k, 0, j]
-            sd[k, j] = down_o[slot]
-            sq[k, j] = q_o[slot]
-            sv[k, j] = v_o[slot]
-        here = pl.multiple_of(g * 2 * rank, 16)
-        remote(sd.at[k], down_f.at[pl.ds(g * 2, 2)], fsem.at[ng - k, 0], peer, t)
-        for j in range(PAIR_MOST):
-            spot = pl.ds(pl.multiple_of((g * 2 + j) * rank, 16), rank)
-            remote(sq.at[k, j], q_f.at[spot, :], fsem.at[ng - k, 1 + j], peer, t)
-            remote(sv.at[k, j], v_f.at[spot, :], fsem.at[ng - k, 3 + j], peer, t)
-
-    wave("A", "x", 1, 0)
-    if nx == 4:
-        launch("A", 1, 0, "z")
-        launch("A", -1, 0, "z")
-    wave("B", "z", 1, 0)
-    for sign in ((-1, 1) if nz > 2 else (1,)):
-        if nz > 1:
-            launch("B", 0, sign, "x")
-    if nx == 4:
-        wave("A", "x", 2, 0)
-        launch("A", 2, 0, "z")
-    elif nx == 2:
-        launch("A", 1, 0, "z")
-
-    loads[6].wait()
-    for k in range(1, nt):
-        arrived(lbuf.at[pl.ds(pl.multiple_of(lax.rem(t + k, nt) * 48, 16), 48), :], lsem.at[k])
-    both = lbuf[...].astype(F32).reshape(nt, 2, 24, 128)
-    xs[...] = jnp.concatenate([both[:, 0], both[:, 1]], axis=-1).reshape(nt * 24, 256)
+    def lend():
+        for load in loads[1:4]:
+            load.wait()
+        down_f[pl.ds(g * 2, 2)] = jnp.zeros((2,) + down_f.shape[1:], BF16)
+        own_spot = pl.ds(pl.multiple_of(g * 2 * rank, 16), 2 * rank)
+        q_f[own_spot, :] = jnp.zeros((2 * rank, q_f.shape[1]), BF16)
+        v_f[own_spot, :] = jnp.zeros((2 * rank, v_f.shape[1]), BF16)
+        for k in range(1, ng):
+            peer = lax.rem(g + k, ng)
+            arrived(rbuf.at[peer], qsem.at[k])
+            down_copy = pltpu.make_async_copy(rbuf.at[peer], rs.at[k], wsem.at[7])
+            down_copy.start()
+            down_copy.wait()
+            for j in range(PAIR_MOST):
+                slot = rs[k, 0, j]
+                sd[k, j] = down_o[slot]
+                sq[k, j] = q_o[slot]
+                sv[k, j] = v_o[slot]
+            remote(sd.at[k], down_f.at[pl.ds(g * 2, 2)], fsem.at[ng - k, 0], peer, t)
+            for j in range(PAIR_MOST):
+                spot = pl.ds(pl.multiple_of((g * 2 + j) * rank, 16), rank)
+                remote(sq.at[k, j], q_f.at[spot, :], fsem.at[ng - k, 1 + j], peer, t)
+                remote(sv.at[k, j], v_f.at[spot, :], fsem.at[ng - k, 3 + j], peer, t)
 
     def shrink(table, first):
         def body(e, carry):
@@ -236,64 +243,99 @@
             return carry
         return body
 
-    part[...] = jnp.zeros(part.shape, F32)
-    lax.fori_loop(0, own, shrink(down_o, 0), 0)
-
-    for k in range(2, nz // 2 + 1):
-        wave("B", "z", k, 0)
-        for sign in ((-1, 1) if k < nz // 2 else (1,)):
-            launch("B", 0, sign * k, "x")
-
-    for k in range(1, ng):
-        peer = lax.rem(g + k, ng)
-        arrived(down_f.at[pl.ds(peer * 2, 2)], fsem.at[k, 0])
-    lax.fori_loop(0, ng * PAIR_MOST, shrink(down_f, own), 0)
-
-    for zz in range(nz):
-        for xx in range(nx):
-            S[xx, zz] = part[pl.ds((zz * nx + xx) * 24, 24), :]
-    for k in range(1, nx):
-        peer = lax.rem(x + k, nx)
-        remote(S.at[peer], pbuf.at[x], p1.at[nx - k], g, z * nx + peer)
-
-    def finish_x(dz):
-        for k in range(1, nx // 2 + 1):
-            wave("B", "x", k, dz)
-
-    def a_wave(k):
-        for dx in range(nx):
-            wave("A", "z", k, dx)
-
-    finish_x(0)
-
-    pbuf[pl.ds(x, 1)] = S[pl.ds(x, 1)]
-    for k in range(1, nx):
-        arrived(pbuf.at[lax.rem(x + k, nx)], p1.at[k])
-    total = pbuf[0]
-    for xx in range(1, nx):
-        total = total + pbuf[xx]
-    pbuf[0] = total
-    for k in range(1, nz):
-        peer = lax.rem(z + k, nz)
-        remote(pbuf.at[0, peer], sbuf.at[z], p2.at[nz - k], g, peer * nx + x)
-
-    if nz > 1:
-        a_wave(1)
-
-    sbuf[pl.ds(z, 1)] = pbuf[0, pl.ds(z, 1)]
-    for k in range(1, nz):
-        arrived(sbuf.at[lax.rem(z + k, nz)], p2.at[k])
-    low = sbuf[0]
-    for zz in range(1, nz):
-        low = low + sbuf[zz]
-    low = jnp.concatenate([low, jnp.zeros((8, 128), F32)], axis=0).astype(BF16)
-    lrz[pl.ds(z, 1)] = low[None]
-    for k in range(1, nz):
-        peer = lax.rem(z + k, nz)
-        remote(lrz.at[z], lrz.at[z], p3.at[nz - k], g, peer * nx + x)
-
-    for load in loads[4:6]:
-        load.wait()
+    def shrink_own():
+        loads[6].wait()
+        for k in range(1, nt):
+            arrived(lbuf.at[pl.ds(pl.multiple_of(lax.rem(t + k, nt) * 48, 16), 48), :], lsem.at[k])
+        both = lbuf[...].astype(F32).reshape(nt, 2, 24, 128)
+        xs[...] = jnp.concatenate([both[:, 0], both[:, 1]], axis=-1).reshape(nt * 24, 256)
+        part[...] = jnp.zeros(part.shape, F32)
+        lax.fori_loop(0, own, shrink(down_o, 0), 0)
+
+    def shrink_far():
+        for k in range(1, ng):
+            peer = lax.rem(g + k, ng)
+            arrived(down_f.at[pl.ds(peer * 2, 2)], fsem.at[k, 0])
+        lax.fori_loop(0, ng * PAIR_MOST, shrink(down_f, own), 0)
+        for zz in range(nz):
+            for xx in range(nx):
+                S[xx, zz] = part[pl.ds((zz * nx + xx) * 24, 24), :]
+        for k in range(1, nx):
+            peer = lax.rem(x + k, nx)
+            remote(S.at[peer], pbuf.at[x], p1.at[nx - k], g, z * nx + peer)
+
+    def sum_x():
+        pbuf[pl.ds(x, 1)] = S[pl.ds(x, 1)]
+        for k in range(1, nx):
+            arrived(pbuf.at[lax.rem(x + k, nx)], p1.at[k])
+        total = pbuf[0]
+        for xx in range(1, nx):
+            total = total + pbuf[xx]
+        pbuf[0] = total
+        for k in range(1, nz):
+            peer = lax.rem(z + k, nz)
+            remote(pbuf.at[0, peer], sbuf.at[z], p2.at[nz - k], g, peer * nx + x)
+
+    def sum_z():
+        sbuf[pl.ds(z, 1)] = pbuf[0, pl.ds(z, 1)]
+        for k in range(1, nz):
+            arrived(sbuf.at[lax.rem(z + k, nz)], p2.at[k])
+        low = sbuf[0]
+        for zz in range(1, nz):
+            low = low + sbuf[zz]
+        low = jnp.concatenate([low, jnp.zeros((8, 128), F32)], axis=0).astype(BF16)
+        lrz[pl.ds(z, 1)] = low[None]
+        for k in range(1, nz):
+            peer = lax.rem(z + k, nz)
+            remote(lrz.at[z], lrz.at[z], p3.at[nz - k], g, peer * nx + x)
+
+    def spread_x():
+        for k in range(1, nz):
+            arrived(lrz.at[lax.rem(z + k, nz)], p3.at[k])
+        lrall[pl.ds(x, 1)] = lrz[...][None]
+        for k in range(1, nx):
+            peer = lax.rem(x + k, nx)
+            remote(lrz, lrall.at[x], p4.at[nx - k], g, z * nx + peer)
+
+    def expand():
+        for k in range(1, nx):
+            arrived(lrall.at[lax.rem(x + k, nx)], p4.at[k])
+        for k in range(1, ng):
+            peer = lax.rem(g + k, ng)
+            for j in range(PAIR_MOST):
+                spot = pl.ds(pl.multiple_of((peer * 2 + j) * rank, 16), rank)
+                arrived(q_f.at[spot, :], fsem.at[k, 1 + j])
+                arrived(v_f.at[spot, :], fsem.at[k, 3 + j])
+
+        for zz in range(nz):
+            for xx in range(nx):
+                low24 = lrall[xx, zz].astype(F32)[:24]
+                spot = pl.ds((zz * nx + xx) * 24, 24)
+                LRq[spot, :] = jnp.concatenate([low24[:, :64], low24[:, :64]], axis=-1)
+                LRv[spot, :] = jnp.concatenate([low24[:, 64:], low24[:, 64:]], axis=-1)
+        Dq[...] = jnp.zeros(Dq.shape, F32)
+        Dv[...] = jnp.zeros(Dv.shape, F32)
+
+        def grow(q_table, v_table, first):
+            def body(i, carry):
+                lane = lax.broadcasted_iota(jnp.int32, (nt * 24, 128), 1) // 64
+                hit0 = tr[...] == lane + (i * 4 + first)
+                hit1 = tr[...] == lane + (i * 4 + 2 + first)
+                spread_q = jnp.concatenate([jnp.where(hit0, LRq[...], 0.0), jnp.where(hit1, LRq[...], 0.0)], axis=-1)
+                spread_v = jnp.concatenate([jnp.where(hit0, LRv[...], 0.0), jnp.where(hit1, LRv[...], 0.0)], axis=-1)
+                Dq[...] += jnp.dot(spread_q.astype(BF16), q_table(i), preferred_element_type=F32)
+                Dv[...] += jnp.dot(spread_v.astype(BF16), v_table(i), preferred_element_type=F32)
+                return carry
+            return body
+
+        def own_table(ref):
+            return lambda i: ref[pl.ds(i * 4, 4)].reshape(4 * rank, ref.shape[2])
+
+        def far_table(ref):
+            return lambda i: ref[pl.ds(pl.multiple_of(i * 4 * rank, 4 * rank), 4 * rank), :]
+
+        lax.fori_loop(0, own // 4, grow(own_table(q_o), own_table(v_o), 0), 0)
+        lax.fori_loop(0, ng * PAIR_MOST // 4, grow(far_table(q_f), far_table(v_f), own), 0)
 
     kt = 512
 
@@ -304,16 +346,18 @@
         def body(k, carry):
             cols = pl.ds(pl.multiple_of(k * kt, kt), kt)
             for h in range(2):
-                acc[h] += jnp.dot(X[rows, cols], wv[h, cols, :], preferred_element_type=F32)
+                acc[h] += lax.dot_general(
+                    X[rows, cols], wv[h, :, cols], (((1,), (1,)), ((), ())), preferred_element_type=F32
+                )
             return carry
 
         lax.fori_loop(0, K2 // kt, body, 0)
         first = acc[0].reshape(nx * 3, 2, 8, NW)[:, 0]
         second = acc[1].reshape(nx * 3, 2, 8, NW)[:, 1]
-        return (first + second).reshape(nx * 24, NW)
+        plain[dz % nz] = (first + second).reshape(nx * 24, NW)
 
     def finish(dz):
-        base = base_of(dz)
+        base = plain[dz % nz]
         zz = lax.rem(z + dz % nz, nz)
         rows = pl.ds(pl.multiple_of(zz * (nx * 24), 8), nx * 24)
         query = base[:, :256] + adapter_scale * Dq[rows, :]
@@ -339,59 +383,43 @@
             else:
                 remote(ob.at[dz % nz, xx], out.at[t], osem.at[(-dx) % nx, (-dz) % nz], g, zz * nx + xx)
 
-    for k in range(1, nz):
-        arrived(lrz.at[lax.rem(z + k, nz)], p3.at[k])
-    lrall[pl.ds(x, 1)] = lrz[...][None]
-    for k in range(1, nx):
-        peer = lax.rem(x + k, nx)
-        remote(lrz, lrall.at[x], p4.at[nx - k], g, z * nx + peer)
-
-    for k in range(1, nx):
-        arrived(lrall.at[lax.rem(x + k, nx)], p4.at[k])
-    for k in range(1, ng):
-        peer = lax.rem(g + k, ng)
-        for j in range(PAIR_MOST):
-            spot = pl.ds(pl.multiple_of((peer * 2 + j) * rank, 16), rank)
-            arrived(q_f.at[spot, :], fsem.at[k, 1 + j])
-            arrived(v_f.at[spot, :], fsem.at[k, 3 + j])
-
-    for zz in range(nz):
-        for xx in range(nx):
-            low24 = lrall[xx, zz].astype(F32)[:24]
-            spot = pl.ds((zz * nx + xx) * 24, 24)
-            LRq[spot, :] = jnp.concatenate([low24[:, :64], low24[:, :64]], axis=-1)
-            LRv[spot, :] = jnp.concatenate([low24[:, 64:], low24[:, 64:]], axis=-1)
-    Dq[...] = jnp.zeros(Dq.shape, F32)
-    Dv[...] = jnp.zeros(Dv.shape, F32)
-
-    def grow(q_table, v_table, first):
-        def body(i, carry):
-            lane = lax.broadcasted_iota(jnp.int32, (nt * 24, 128), 1) // 64
-            hit0 = tr[...] == lane + (i * 4 + first)
-            hit1 = tr[...] == lane + (i * 4 + 2 + first)
-            spread_q = jnp.concatenate([jnp.where(hit0, LRq[...], 0.0), jnp.where(hit1, LRq[...], 0.0)], axis=-1)
-            spread_v = jnp.concatenate([jnp.where(hit0, LRv[...], 0.0), jnp.where(hit1, LRv[...], 0.0)], axis=-1)
-            Dq[...] += jnp.dot(spread_q.astype(BF16), q_table(i), preferred_element_type=F32)
-            Dv[...] += jnp.dot(spread_v.astype(BF16), v_table(i), preferred_element_type=F32)
-            return carry
-        return body
-
-    def own_table(ref):
-        return lambda i: ref[pl.ds(i * 4, 4)].reshape(4 * rank, ref.shape[2])
-
-    def far_table(ref):
-        return lambda i: ref[pl.ds(pl.multiple_of(i * 4 * rank, 4 * rank), 4 * rank), :]
-
-    lax.fori_loop(0, own // 4, grow(own_table(q_o), own_table(v_o), 0), 0)
-    lax.fori_loop(0, ng * PAIR_MOST // 4, grow(far_table(q_f), far_table(v_f), own), 0)
-
-    finish(0)
-    for k in range(1, nz // 2 + 1):
-        if k > 1:
-            a_wave(k)
-        for sign in ((-1, 1) if k < nz // 2 else (1,)):
-            finish_x(sign * k)
-            finish(sign * k)
+    chores = [
+        (CHORES[0], lend), (CHORES[1], shrink_own), (CHORES[2], shrink_far), (CHORES[3], sum_x),
+        (CHORES[4], sum_z), (CHORES[5], spread_x), (CHORES[6], expand),
+    ]
+    loaded = []
+    ready = []
+    based = []
+    missing = {dz: 2 * nx for dz in range(nz)}
+    missing[0] -= 2
+
+    def settle(now):
+        while chores and chores[0][0] <= now:
+            chores.pop(0)[1]()
+        while ready:
+            if not loaded:
+                for load in loads[4:6]:
+                    load.wait()
+                loaded.append(1)
+            dz = ready.pop(0)
+            base_of(dz)
+            based.append(dz)
+        while based and not chores:
+            finish(based.pop(0))
+
+    for kind, when, name, dx, dz, half in ring_order(nx, nz, LA, LB):
+        if kind == "send":
+            axis, step = when
+            forward(name, dx, dz, half, axis, step)
+        else:
+            settle(when)
+            piece_half, last = (None, True) if half is None else half
+            expect(name, dx, dz, piece_half)
+            if last:
+                missing[dz] -= 1
+                if missing[dz] == 0:
+                    ready.append(dz)
+    settle(1e9)
 
     for dz in range(nz):
         for dx in range(nx):
@@ -405,7 +433,7 @@
     nt = nx * nz
     K2 = xk.shape[1]
     own = down.shape[0]
-    NW = w.shape[1]
+    NW = w.shape[0]
     DMA = pltpu.SemaphoreType.DMA
     vmem = pl.BlockSpec(memory_space=pltpu.VMEM)
     hbm = pl.BlockSpec(memory_space=pl.ANY)
@@ -418,7 +446,7 @@
         out_specs=vmem,
         scratch_shapes=[
             pltpu.VMEM((nt * 48, K2), BF16),
-            pltpu.VMEM((2, K2, NW), BF16),
+            pltpu.VMEM((2, NW, K2), BF16),
             pltpu.VMEM((nt * 48, 128), BF16),
             pltpu.VMEM((rows, 256), F32),
             pltpu.VMEM(down.shape, BF16),
@@ -443,6 +471,7 @@
             pltpu.VMEM((rows, 256), F32),
             pltpu.VMEM((rows, 128), F32),
             pltpu.VMEM((2, nx * 48, NW), F32),
+            pltpu.VMEM((nz, nx * 24, NW), F32),
             pltpu.VMEM((nz, nx, 64, 128), BF16),
             DMA((sends,)),
             DMA((2, nx, nz, 2)),
@@ -470,31 +499,39 @@
     kv_width = hist.shape[2] // 2
     length = lengths[row]
     factor = HEAD_DIM ** (-0.5)
-    past_live = lax.broadcasted_iota(jnp.int32, (32, window), 1) < length
-    step = lax.broadcasted_iota(jnp.int32, (32, 16), 0) // 8
-    fresh_at = lax.broadcasted_iota(jnp.int32, (32, 16), 1)
-    fresh_live = jnp.logical_and(fresh_at <= step, fresh_at < 3)
+    past_live = lax.broadcasted_iota(jnp.int32, (KV_HEADS * 32, window), 1) < length
+    at = lax.broadcasted_iota(jnp.int32, (KV_HEADS * 32, KV_HEADS * 16), 0)
+    fresh_at = lax.broadcasted_iota(jnp.int32, (KV_HEADS * 32, KV_HEADS * 16), 1)
+    same_head = at // 32 == fresh_at // 16
+    order = fresh_at % 16
+    fresh_live = jnp.logical_and(same_head, jnp.logical_and(order <= (at % 32) // 8, order < 3))
+    dims = (((1,), (1,)), ((), ()))
+    past = []
     for h in range(KV_HEADS):
         keys = hist[0, :, h * HEAD_DIM : (h + 1) * HEAD_DIM]
+        past.append(lax.dot_general(q[0, h], keys, dims, preferred_element_type=F32))
+    past = jnp.concatenate(past, axis=0) * factor
+    queries = q[0].reshape(KV_HEADS * 32, HEAD_DIM)
+    fresh_keys = fk[0].reshape(KV_HEADS * 16, HEAD_DIM)
+    fresh_values = fv[0].reshape(KV_HEADS * 16, HEAD_DIM)
+    fresh = lax.dot_general(queries, fresh_keys, dims, preferred_element_type=F32) * factor
+    past = jnp.where(past_live, past, -jnp.inf)
+    fresh = jnp.where(fresh_live, fresh, -jnp.inf)
+    highest = jnp.maximum(
+        jnp.max(past, axis=-1, keepdims=True), jnp.max(fresh, axis=-1, keepdims=True)
+    )
+    past = jnp.exp(past - highest)
+    fresh = jnp.exp(fresh - highest)
+    total = jnp.sum(past, axis=-1, keepdims=True) + jnp.sum(fresh, axis=-1, keepdims=True)
+    past = (past / total).astype(BF16)
+    fresh = (fresh / total).astype(BF16)
+    context = jnp.dot(fresh, fresh_values, preferred_element_type=F32)
+    for h in range(KV_HEADS):
         values = hist[0, :, kv_width + h * HEAD_DIM : kv_width + (h + 1) * HEAD_DIM]
-        queries = q[0, h]
-        dims = (((1,), (1,)), ((), ()))
-        past = lax.dot_general(queries, keys, dims, preferred_element_type=F32) * factor
-        fresh = lax.dot_general(queries, fk[0, h], dims, preferred_element_type=F32) * factor
-        past = jnp.where(past_live, past, -jnp.inf)
-        fresh = jnp.where(fresh_live, fresh, -jnp.inf)
-        highest = jnp.maximum(
-            jnp.max(past, axis=-1, keepdims=True), jnp.max(fresh, axis=-1, keepdims=True)
-        )
-        past = jnp.exp(past - highest)
-        fresh = jnp.exp(fresh - highest)
-        total = jnp.sum(past, axis=-1, keepdims=True) + jnp.sum(fresh, axis=-1, keepdims=True)
-        past = (past / total).astype(BF16)
-        fresh = (fresh / total).astype(BF16)
-        context = jnp.dot(past, values, preferred_element_type=F32) + jnp.dot(
-            fresh, fv[0, h], preferred_element_type=F32
-        )
-        out[0, h] = context.astype(BF16)
+        rows = slice(h * 32, (h + 1) * 32)
+        out[0, h] = (
+            context[rows] + jnp.dot(past[rows], values, preferred_element_type=F32)
+        ).astype(BF16)
 
 
 def attend(lengths, q, fk, fv, hist):
@@ -511,7 +548,7 @@
             pl.BlockSpec((1, window, width), lambda r: (r, 0, 0)),
         ],
         out_specs=pl.BlockSpec((1, KV_HEADS, 32, HEAD_DIM), lambda r: (r, 0, 0, 0)),
-        compiler_params=pltpu.CompilerParams(vmem_limit_bytes=32 * MIB),
+        compiler_params=pltpu.CompilerParams(vmem_limit_bytes=56 * MIB),
         name="attend",
     )(lengths, q, fk, fv, hist)
 
@@ -558,7 +595,7 @@
     tr = jnp.broadcast_to(table_row.reshape(nt, 1, rows_here, 1), (nt, steps, rows_here, 128))
     tr = tr.reshape(nt * steps * rows_here, 128)
     vpad = jnp.pad(value_up, ((0, 0), (0, 0), (32, 64)))
-    return project(nx, nz, ng, xk, xl, united_weight, adapter_down, query_up, vpad, req, tr)
+    return project(nx, nz, ng, xk, xl, united_weight.T, adapter_down, query_up, vpad, req, tr)
 
 
 def local(

time: 229 us -> 152 us (0.66)
  Pallas kernels: 200 us -> 131 us
  local copies, waits for them, and re-layouts: 20.6 us -> 12.2 us
    pallas_call x1, Pallas kernels: 176 us -> 121 us  [project(): pl.pallas_call(functools.partial(project_kernel, nx, nz, ng, own), out_sh...]
    pallas_call x1, Pallas kernels: 23.7 us -> 9.94 us  [attend(): pl.pallas_call(attend_kernel, out_shape=jax.ShapeDtypeStruct((rows, KV_HE...]
    unnamed x9 -> x6, local copies, waits for them, and re-layouts: 11.9 us -> 1.23 us
where the time goes in v2:
time: 152 us; the launch traced here: 151 us
  Pallas kernels  131 us (86%)
  local copies, waits for them, and re-layouts  12.2 us (8%)
  other arithmetic  7.68 us (5%)
    pallas_call x1, Pallas kernels, project(): pl.pallas_call(functools.partial(project_kernel, nx, nz, ng, own), out_sh...  121 us
    pallas_call x1, Pallas kernels, attend(): pl.pallas_call(attend_kernel, out_shape=jax.ShapeDtypeStruct((rows, KV_HE...  9.94 us

profile of v2, /device:TPU:8, one launch (start us, length us, event | category | flops | bytes accessed | tf_op | source)
XLA Modules:
  0.0 151.5 jit_solution(12600598767661798814)
XLA Ops:
  0.0 0.8 select_reduce_fusion.1
  0.8 0.1 fusion.5
  0.9 0.1 reshape.200
  1.0 0.1 fusion.13
  1.1 0.2 reduce_window_sum.13
  1.3 0.1 reduce_window_sum.14
  1.4 0.1 and.49
  1.4 0.1 and.55
  1.5 0.1 select_reduce_fusion
  1.7 0.1 reduce_sum.42
  1.8 0.1 div.18
  1.8 0.1 rem.24
  2.0 0.1 ne.53
  2.1 0.1 broadcast_in_dim.67
  2.2 0.9 broadcast_in_dim.68.tr
  3.1 0.1 select_reduce_fusion.2
  3.3 0.1 copy.47
  3.4 0.6 pad.20.req
  4.0 0.7 convert_element_type.67
  4.7 1.2 fusion
  5.9 1.2 fusion.16
  7.1 0.1 copy.61
  7.2 1.0 copy.45
  8.2 1.9 %fusion.2 = bf16[3,8,8192]{2,1,0:T(8,128)(2,1)} fusion(bf16[3,8,8192]{2,1,0:T(8,128)(2,1)} %param.10, f32[8192]{0:T(1024)S(1)} %convert_element_type.67, f32[3,8]{1,0:T(4,128)S(1)} %add_rsqrt_fusion), kind=kLoop, calls=%fused_computation.4 | loop fusion | flops 786432 | bytes 819296 | tf_op jit(solution)/shard_map/convert_element_type | solution.py:29
  10.1 1.1 copy.46
  11.2 0.9 pad.19.vup
  12.2 121.5 %project.1 = bf16[32,64,128]{2,1,0:T(8,128)(2,1)} custom-call(bf16[48,4096]{1,0:T(8,128)(2,1)} %bitcast.51, bf16[1536,128]{1,0:T(8,128)(2,1)} %bitcast.50, bf16[320,8192]{1,0:T(8,128)(2,1)} %bitcast.48, bf16[24,256,128]{2,1,0:T(8,128)(2,1)} %down.1, bf16[24,64,256]{2,1,0:T(8,128)(2,1)} %qup.1, bf16[24,64,128]{2,1,0:T(8,128)(2,1)} %pad.19.vup, ...), custom_call_target="tpu_custom_call" | custom-call | tf_op jit(solution)/shard_map/project/pallas_call | solution.py:442
  133.6 1.0 slice.33
  134.6 0.1 reshape.202
  134.8 0.1 fusion.14
  135.0 0.1 copy.51
  135.0 0.1 reshape.208
  135.2 0.1 fusion.15
  135.3 0.1 dynamic_slice.3.lengths
  135.4 0.1 multiply_cosine_fusion
  135.5 0.2 fusion.7
  135.7 0.1 maximum_bitcast_fusion.1
  135.8 0.7 pad.22.fk
  136.6 0.1 convert_bitcast_fusion
  136.6 0.4 copy.48
  137.0 0.4 fusion.3
  137.4 0.2 copy_bitcast_fusion
  137.7 0.9 pad.21.q
  138.5 0.1 reshape.204
  138.7 0.8 pad.23.fv
  139.5 9.9 %attend.1 = bf16[8,8,32,128]{3,2,1,0:T(8,128)(2,1)} custom-call(s32[8]{0:T(128)} %copy-done, bf16[8,8,32,128]{3,2,1,0:T(8,128)(2,1)} %pad.21.q, bf16[8,8,16,128]{3,2,1,0:T(8,128)(2,1)} %pad.22.fk, bf16[8,8,16,128]{3,2,1,0:T(8,128)(2,1)} %pad.23.fv, bf16[8,256,2048]{2,1,0:T(8,128)(2,1)} %hist.1), custom_call_target="tpu_custom_call" | custom-call | tf_op jit(solution)/shard_map/attend/pallas_call | solution.py:539
  149.5 1.0 slice_bitcast_fusion
  150.5 1.0 copy.58
  (22 shorter events, 0.3 us)
Async XLA Ops:
  12.2 123.1 %copy-start.1 = (s32[256]{0:T(256)S(1)}, s32[256]{0:T(256)}, u32[]{:S(2)}) copy-start(s32[256]{0:T(256)} %param.19) | copy-start | bytes 3076
  133.6 2.9 %slice-start = ((bf16[32,64,128]{2,1,0:T(8,128)(2,1)}), bf16[32,48,128]{2,1,0:T(8,128)(2,1)S(1)}, s32[]{:S(2)}) async-start(bf16[32,64,128]{2,1,0:T(8,128)(2,1)} %project.1), calls=%async_computation | async-start | bytes 786432 | tf_op jit(solution)/shard_map/slice | solution.py:612
  135.4 4.1 %copy-start = (s32[8]{0:T(128)}, s32[8]{0:T(128)S(1)}, u32[]{:S(2)}) copy-start(s32[8]{0:T(128)S(1)} %dynamic_slice.3.lengths) | copy-start | bytes 100

commit v3 on v2

--- a/solution.py
+++ b/solution.py
@@ -23,30 +23,17 @@
 MESH = pl.DeviceIdType.MESH
 
 
-def rms_normed(inputs, norm_gain):
-    values = inputs.astype(F32)
-    mean_square = jnp.mean(values * values, axis=-1, keepdims=True)
-    return (values * lax.rsqrt(mean_square + norm_eps) * norm_gain.astype(F32)).astype(BF16)
-
-
-def rotate(heads_in, positions):
-    head_width = heads_in.shape[-1]
-    halfway = head_width // 2
-    ladder = jnp.arange(halfway).astype(F32) * (2.0 / head_width)
+def rope_tables(positions):
+    halfway = HEAD_DIM // 2
+    ladder = jnp.arange(halfway).astype(F32) * (2.0 / HEAD_DIM)
     inverse = jnp.power(F32(rope_base), -ladder)
-    angles = positions.astype(F32)[..., None, None] * inverse
+    angles = positions.astype(F32)[:, None] * inverse[None, :]
     cosine = jnp.cos(angles)
-    sine_part = jnp.sin(angles)
-    values = heads_in.astype(F32)
-    leading = values[..., :halfway]
-    trailing = values[..., halfway:]
-    turned = jnp.concatenate(
-        [leading * cosine - trailing * sine_part, trailing * cosine + leading * sine_part], axis=-1
-    )
-    return turned.astype(BF16)
-
-
-CHORES = (3.0, 18.0, 50.0, 57.0, 63.0, 68.0, 73.0)
+    sine = jnp.sin(angles)
+    return jnp.concatenate([cosine, cosine], axis=-1), jnp.concatenate([-sine, sine], axis=-1)
+
+
+CHORES = (3.0, 16.0, 32.0, 46.0, 56.0, 66.0, 75.0)
 BUSY = {"x": 4.0, "z": 8.0}
 RATE = 45e3
 
@@ -106,10 +93,10 @@
 
 def project_kernel(
     nx, nz, ng, own,
-    xk, xl, w, down, qup, vup, req, tr,
+    inputs, gain, w, down, qup, vup, req, spot_of_row,
     out,
-    X, wv, lbuf, xs, down_o, q_o, v_o, down_f, q_f, v_f, sd, sq, sv, rbuf, rs,
-    part, pbuf, S, sbuf, lrz, lrall, LRq, LRv, Dq, Dv, acc, plain, ob,
+    X, xl, tr, wv, vraw, lbuf, xs, down_o, q_o, v_o, down_f, q_f, v_f, sd, sq, sv, rbuf, rsend, rs,
+    part, pbuf, S, half_sum, sbuf, lrz, lrall, LRq, LRv, Dq, Dv, acc, plain, ob,
     ssem, gsem, lsem, dsem, fsem, qsem, p1, p2, p3, p4, osem, wsem,
 ):
     nt = nx * nz
@@ -167,17 +154,29 @@
 
     mine = pl.multiple_of(t * 48, 16)
     loads = [
-        pltpu.make_async_copy(xk, X.at[pl.ds(mine, 48), :], wsem.at[0]),
         pltpu.make_async_copy(down, down_o, wsem.at[1]),
         pltpu.make_async_copy(qup, q_o, wsem.at[2]),
-        pltpu.make_async_copy(vup, v_o, wsem.at[3]),
+        pltpu.make_async_copy(vup, vraw, wsem.at[3]),
         pltpu.make_async_copy(w.at[:, pl.ds(0, K2)], wv.at[0], wsem.at[4]),
         pltpu.make_async_copy(w.at[:, pl.ds(K2, K2)], wv.at[1], wsem.at[5]),
-        pltpu.make_async_copy(xl.at[pl.ds(mine, 48), :], lbuf.at[pl.ds(mine, 48), :], wsem.at[6]),
     ]
     for load in loads:
         load.start()
-    loads[0].wait()
+
+    values = inputs[...].astype(F32)
+    mean_square = jnp.mean(values * values, axis=-1, keepdims=True)
+    normed = values * lax.rsqrt(mean_square + norm_eps) * gain[...].astype(F32).reshape(1, 1, 2 * K2)
+    for step in range(3):
+        halves = jnp.concatenate([normed[step, :, :K2], normed[step, :, K2:]], axis=0)
+        X[pl.ds(pl.multiple_of(mine + step * 16, 16), 16), :] = halves.astype(BF16)
+    for p in range(nt):
+        pieces = [normed[step, :, p * 256 + h * 128 : p * 256 + h * 128 + 128] for h in range(2) for step in range(3)]
+        xl[p * 48 : p * 48 + 48, :] = jnp.concatenate(pieces, axis=0).astype(BF16)
+    lbuf[pl.ds(mine, 48), :] = xl[pl.ds(mine, 48), :]
+    rsend[...] = jnp.zeros((8, 128), jnp.int32)
+    rsend[0:ng, 0:PAIR_MOST] = req[...]
+    spots = jnp.broadcast_to(spot_of_row[...], (nt * 8, 128)).reshape(nt, 1, 8, 128)
+    tr[...] = jnp.broadcast_to(spots, (nt, 3, 8, 128)).reshape(nt * 24, 128)
 
     pl.semaphore_wait(barrier, nt - 1 + ng - 1)
 
@@ -208,11 +207,19 @@
         )
     for k in range(1, ng):
         peer = lax.rem(g + k, ng)
-        remote(req.at[peer], rbuf.at[g], qsem.at[ng - k], peer, t)
+        remote(rsend, rbuf.at[g], qsem.at[ng - k], peer, t)
 
     def lend():
-        for load in loads[1:4]:
+        for load in loads[0:3]:
             load.wait()
+        def turn(e, carry):
+            column = vraw[e].astype(F32).T
+            left = jnp.zeros((rank, 32), F32)
+            right = jnp.zeros((rank, 64), F32)
+            v_o[e] = jnp.concatenate([left, column, right], axis=-1).astype(BF16)
+            return carry
+
+        lax.fori_loop(0, own, turn, 0)
         down_f[pl.ds(g * 2, 2)] = jnp.zeros((2,) + down_f.shape[1:], BF16)
         own_spot = pl.ds(pl.multiple_of(g * 2 * rank, 16), 2 * rank)
         q_f[own_spot, :] = jnp.zeros((2 * rank, q_f.shape[1]), BF16)
@@ -224,7 +231,7 @@
             down_copy.start()
             down_copy.wait()
             for j in range(PAIR_MOST):
-                slot = rs[k, 0, j]
+                slot = rs[k, g, j]
                 sd[k, j] = down_o[slot]
                 sq[k, j] = q_o[slot]
                 sv[k, j] = v_o[slot]
@@ -244,7 +251,6 @@
         return body
 
     def shrink_own():
-        loads[6].wait()
         for k in range(1, nt):
             arrived(lbuf.at[pl.ds(pl.multiple_of(lax.rem(t + k, nt) * 48, 16), 48), :], lsem.at[k])
         both = lbuf[...].astype(F32).reshape(nt, 2, 24, 128)
@@ -257,9 +263,9 @@
             peer = lax.rem(g + k, ng)
             arrived(down_f.at[pl.ds(peer * 2, 2)], fsem.at[k, 0])
         lax.fori_loop(0, ng * PAIR_MOST, shrink(down_f, own), 0)
-        for zz in range(nz):
-            for xx in range(nx):
-                S[xx, zz] = part[pl.ds((zz * nx + xx) * 24, 24), :]
+        whole_part = part[...].reshape(nz, nx, 24, 128)
+        for xx in range(nx):
+            S[xx] = whole_part[:, xx].reshape(nz * 24, 128).astype(BF16)
         for k in range(1, nx):
             peer = lax.rem(x + k, nx)
             remote(S.at[peer], pbuf.at[x], p1.at[nx - k], g, z * nx + peer)
@@ -268,23 +274,24 @@
         pbuf[pl.ds(x, 1)] = S[pl.ds(x, 1)]
         for k in range(1, nx):
             arrived(pbuf.at[lax.rem(x + k, nx)], p1.at[k])
-        total = pbuf[0]
+        total = pbuf[0].astype(F32)
         for xx in range(1, nx):
-            total = total + pbuf[xx]
-        pbuf[0] = total
+            total = total + pbuf[xx].astype(F32)
+        blank = jnp.zeros((8, 128), F32)
+        for zz in range(nz):
+            half_sum[zz] = jnp.concatenate([total[zz * 24 : zz * 24 + 24], blank], axis=0).astype(BF16)
         for k in range(1, nz):
             peer = lax.rem(z + k, nz)
-            remote(pbuf.at[0, peer], sbuf.at[z], p2.at[nz - k], g, peer * nx + x)
+            remote(half_sum.at[peer], sbuf.at[z], p2.at[nz - k], g, peer * nx + x)
 
     def sum_z():
-        sbuf[pl.ds(z, 1)] = pbuf[0, pl.ds(z, 1)]
+        sbuf[pl.ds(z, 1)] = half_sum[pl.ds(z, 1)]
         for k in range(1, nz):
             arrived(sbuf.at[lax.rem(z + k, nz)], p2.at[k])
-        low = sbuf[0]
+        low = sbuf[0].astype(F32)
         for zz in range(1, nz):
-            low = low + sbuf[zz]
-        low = jnp.concatenate([low, jnp.zeros((8, 128), F32)], axis=0).astype(BF16)
-        lrz[pl.ds(z, 1)] = low[None]
+            low = low + sbuf[zz].astype(F32)
+        lrz[pl.ds(z, 1)] = low.astype(BF16)[None]
         for k in range(1, nz):
             peer = lax.rem(z + k, nz)
             remote(lrz.at[z], lrz.at[z], p3.at[nz - k], g, peer * nx + x)
@@ -398,7 +405,7 @@
             chores.pop(0)[1]()
         while ready:
             if not loaded:
-                for load in loads[4:6]:
+                for load in loads[3:5]:
                     load.wait()
                 loaded.append(1)
             dz = ready.pop(0)
@@ -429,9 +436,9 @@
         copy.wait_send()
 
 
-def project(nx, nz, ng, xk, xl, w, down, qup, vup, req, tr):
+def project(nx, nz, ng, inputs, gain, w, down, qup, vup, req, spot_of_row):
     nt = nx * nz
-    K2 = xk.shape[1]
+    K2 = inputs.shape[2] // 2
     own = down.shape[0]
     NW = w.shape[0]
     DMA = pltpu.SemaphoreType.DMA
@@ -446,12 +453,15 @@
         out_specs=vmem,
         scratch_shapes=[
             pltpu.VMEM((nt * 48, K2), BF16),
+            pltpu.VMEM((nt * 48, 128), BF16),
+            pltpu.VMEM((rows, 128), jnp.int32),
             pltpu.VMEM((2, NW, K2), BF16),
+            pltpu.VMEM(vup.shape, BF16),
             pltpu.VMEM((nt * 48, 128), BF16),
             pltpu.VMEM((rows, 256), F32),
             pltpu.VMEM(down.shape, BF16),
             pltpu.VMEM(qup.shape, BF16),
-            pltpu.VMEM(vup.shape, BF16),
+            pltpu.VMEM((own, 64, 128), BF16),
             pltpu.VMEM((ng * 2,) + down.shape[1:], BF16),
             pltpu.VMEM((ng * 2 * 64, 256), BF16),
             pltpu.VMEM((ng * 2 * 64, 128), BF16),
@@ -459,11 +469,13 @@
             pltpu.VMEM((ng, 2, 64, 256), BF16),
             pltpu.VMEM((ng, 2, 64, 128), BF16),
             pltpu.VMEM((ng, 8, 128), jnp.int32),
+            pltpu.VMEM((8, 128), jnp.int32),
             pltpu.SMEM((ng, 8, 128), jnp.int32),
             pltpu.VMEM((rows, 128), F32),
-            pltpu.VMEM((nx, nz, 24, 128), F32),
-            pltpu.VMEM((nx, nz, 24, 128), F32),
-            pltpu.VMEM((nz, 24, 128), F32),
+            pltpu.VMEM((nx, nz * 24, 128), BF16),
+            pltpu.VMEM((nx, nz * 24, 128), BF16),
+            pltpu.VMEM((nz, 32, 128), BF16),
+            pltpu.VMEM((nz, 32, 128), BF16),
             pltpu.VMEM((nz, 32, 128), BF16),
             pltpu.VMEM((nx, nz, 32, 128), BF16),
             pltpu.VMEM((rows, 128), F32),
@@ -490,32 +502,67 @@
             collective_id=0, has_side_effects=True, vmem_limit_bytes=56 * MIB
         ),
         name="project",
-    )(xk, xl, w, down, qup, vup, req, tr)
-
-
-def attend_kernel(lengths, q, fk, fv, hist, out):
-    row = pl.program_id(0)
-    window = hist.shape[1]
-    kv_width = hist.shape[2] // 2
-    length = lengths[row]
+    )(inputs, gain, w, down, qup, vup, req, spot_of_row)
+
+
+def attend_kernel(lengths, got, cos, sin, keys, values, out, scr, res):
+    rows_here, window, _ = keys.shape
     factor = HEAD_DIM ** (-0.5)
-    past_live = lax.broadcasted_iota(jnp.int32, (KV_HEADS * 32, window), 1) < length
-    at = lax.broadcasted_iota(jnp.int32, (KV_HEADS * 32, KV_HEADS * 16), 0)
-    fresh_at = lax.broadcasted_iota(jnp.int32, (KV_HEADS * 32, KV_HEADS * 16), 1)
-    same_head = at // 32 == fresh_at // 16
-    order = fresh_at % 16
-    fresh_live = jnp.logical_and(same_head, jnp.logical_and(order <= (at % 32) // 8, order < 3))
     dims = (((1,), (1,)), ((), ()))
+    lane = lax.broadcasted_iota(jnp.int32, (8, 128), 1) // 32
+
+    def turned(v, c, n):
+        return v * c + pltpu.roll(v, 64, 1) * n
+
+    for b in range(8):
+        block = got[b].astype(F32)
+        for hh in range(2):
+            scr[b, hh * 24 : hh * 24 + 24, :] = turned(block[hh * 24 : hh * 24 + 24], cos[...], sin[...])
+        scr[b, 48:64, :] = block[48:64]
+
+    def gathered(head, row, offset):
+        total = jnp.zeros((8, 128), F32)
+        for b in range(4):
+            moved = pltpu.roll(scr[4 * head + b, row : row + 8, :], (32 * b - offset) % 128, 1)
+            total = jnp.where(lane == b, moved, total)
+        return total
+
+    pad = jnp.zeros((8, 128), F32)
+    fresh_keys = []
+    fresh_values = []
+    for e in range(2):
+        new = [gathered(e, 48, 0), gathered(e, 48, 64), gathered(e, 56, 0)]
+        new = turned(jnp.concatenate(new, axis=0), cos[...], sin[...])
+        fresh_keys.append(jnp.concatenate([new, pad], axis=0))
+        new = [gathered(e, 48, 32), gathered(e, 48, 96), gathered(e, 56, 32), pad]
+        fresh_values.append(jnp.concatenate(new, axis=0))
+    fresh_keys = jnp.concatenate(fresh_keys, axis=-1).astype(BF16)
+    fresh_values = jnp.concatenate(fresh_values, axis=-1).astype(BF16)
+
+    blank = jnp.zeros((32, 128), F32)
+    column = lax.broadcasted_iota(jnp.int32, (64, window), 1)
+    queries = []
     past = []
-    for h in range(KV_HEADS):
-        keys = hist[0, :, h * HEAD_DIM : (h + 1) * HEAD_DIM]
-        past.append(lax.dot_general(q[0, h], keys, dims, preferred_element_type=F32))
-    past = jnp.concatenate(past, axis=0) * factor
-    queries = q[0].reshape(KV_HEADS * 32, HEAD_DIM)
-    fresh_keys = fk[0].reshape(KV_HEADS * 16, HEAD_DIM)
-    fresh_values = fv[0].reshape(KV_HEADS * 16, HEAD_DIM)
+    for r in range(rows_here):
+        q = [
+            jnp.concatenate([scr[4 * e + b, pl.ds(r, 8, stride=8), :] for b in range(4)], axis=0)
+            for e in range(2)
+        ]
+        q = jnp.concatenate(
+            [jnp.concatenate([q[0], blank], axis=-1), jnp.concatenate([blank, q[1]], axis=-1)], axis=0
+        ).astype(BF16)
+        queries.append(q)
+        score = lax.dot_general(q, keys[r], dims, preferred_element_type=F32) * factor
+        past.append(jnp.where(column < lengths[r], score, -jnp.inf))
+    queries = jnp.concatenate(queries, axis=0)
+    past = jnp.concatenate(past, axis=0)
     fresh = lax.dot_general(queries, fresh_keys, dims, preferred_element_type=F32) * factor
-    past = jnp.where(past_live, past, -jnp.inf)
+    at = lax.broadcasted_iota(jnp.int32, fresh.shape, 0)
+    fresh_at = lax.broadcasted_iota(jnp.int32, fresh.shape, 1)
+    order = at % 8
+    step = jnp.where(order >= 3, order - 3, order)
+    own_row = at // 64 == fresh_at % 8
+    fresh_live = jnp.logical_and(own_row, jnp.logical_and(fresh_at // 8 <= step, fresh_at < 24))
     fresh = jnp.where(fresh_live, fresh, -jnp.inf)
     highest = jnp.maximum(
         jnp.max(past, axis=-1, keepdims=True), jnp.max(fresh, axis=-1, keepdims=True)
@@ -526,31 +573,42 @@
     past = (past / total).astype(BF16)
     fresh = (fresh / total).astype(BF16)
     context = jnp.dot(fresh, fresh_values, preferred_element_type=F32)
-    for h in range(KV_HEADS):
-        values = hist[0, :, kv_width + h * HEAD_DIM : kv_width + (h + 1) * HEAD_DIM]
-        rows = slice(h * 32, (h + 1) * 32)
-        out[0, h] = (
-            context[rows] + jnp.dot(past[rows], values, preferred_element_type=F32)
-        ).astype(BF16)
-
-
-def attend(lengths, q, fk, fv, hist):
+    for r in range(rows_here):
+        rows = slice(r * 64, (r + 1) * 64)
+        part = context[rows] + jnp.dot(past[rows], values[r], preferred_element_type=F32)
+        for e in range(2):
+            for b in range(4):
+                res[4 * e + b, r * 8 : r * 8 + 8, :] = part[
+                    32 * e + b * 8 : 32 * e + b * 8 + 8, 128 * e : 128 * e + 128
+                ]
+    for b in range(8):
+        for hh in range(2):
+            for k in range(3):
+                spot = slice((2 * b + hh) * 128, (2 * b + hh) * 128 + 128)
+                out[k, :, spot] = res[b, pl.ds(hh * 3 + k, 8, stride=8), :].astype(BF16)
+
+
+def attend(lengths, got, cos, sin, hist):
     rows, window, width = hist.shape
+    steps = cos.shape[0] // rows
+    pairs = got.shape[0] // 8
     return pl.pallas_call(
         attend_kernel,
-        out_shape=jax.ShapeDtypeStruct((rows, KV_HEADS, 32, HEAD_DIM), BF16),
-        grid=(rows,),
+        out_shape=jax.ShapeDtypeStruct((steps, rows, HEADS * HEAD_DIM), BF16),
+        grid=(pairs,),
         in_specs=[
             pl.BlockSpec(memory_space=pltpu.SMEM),
-            pl.BlockSpec((1, KV_HEADS, 32, HEAD_DIM), lambda r: (r, 0, 0, 0)),
-            pl.BlockSpec((1, KV_HEADS, 16, HEAD_DIM), lambda r: (r, 0, 0, 0)),
-            pl.BlockSpec((1, KV_HEADS, 16, HEAD_DIM), lambda r: (r, 0, 0, 0)),
-            pl.BlockSpec((1, window, width), lambda r: (r, 0, 0)),
+            pl.BlockSpec((8, 64, 128), lambda h: (h, 0, 0)),
+            pl.BlockSpec((steps * rows, 128), lambda h: (0, 0)),
+            pl.BlockSpec((steps * rows, 128), lambda h: (0, 0)),
+            pl.BlockSpec((rows, window, 2 * HEAD_DIM), lambda h: (0, 0, h)),
+            pl.BlockSpec((rows, window, 2 * HEAD_DIM), lambda h: (0, 0, KV_HEADS // 2 + h)),
         ],
-        out_specs=pl.BlockSpec((1, KV_HEADS, 32, HEAD_DIM), lambda r: (r, 0, 0, 0)),
+        out_specs=pl.BlockSpec((steps, rows, 2 * HEADS // KV_HEADS * HEAD_DIM), lambda h: (0, 0, h)),
+        scratch_shapes=[pltpu.VMEM((8, 64, 128), F32), pltpu.VMEM((8, 64, 128), F32)],
         compiler_params=pltpu.CompilerParams(vmem_limit_bytes=56 * MIB),
         name="attend",
-    )(lengths, q, fk, fv, hist)
+    )(lengths, got, cos, sin, hist, hist)
 
 
 def routing(adapter_slot, row_adapter, store, groups, home):
@@ -586,16 +644,11 @@
     nx = NX
     nz = nt // nx
     g = lax.axis_index("group")
-    half = width // 2
     request, table_row = routing(adapter_slot, row_adapter, adapter_down.shape[0], ng, g)
-    normed = rms_normed(inputs, norm_gain)
-    xk = normed.reshape(steps, rows_here, 2, half).transpose(0, 2, 1, 3).reshape(steps * 2 * rows_here, half)
-    xl = normed.reshape(steps * rows_here, nt * 2, 128).transpose(1, 0, 2).reshape(nt * 48, 128)
-    req = jnp.pad(request[:, None, :], ((0, 0), (0, 7), (0, 128 - PAIR_MOST)))
-    tr = jnp.broadcast_to(table_row.reshape(nt, 1, rows_here, 1), (nt, steps, rows_here, 128))
-    tr = tr.reshape(nt * steps * rows_here, 128)
-    vpad = jnp.pad(value_up, ((0, 0), (0, 0), (32, 64)))
-    return project(nx, nz, ng, xk, xl, united_weight.T, adapter_down, query_up, vpad, req, tr)
+    return project(
+        nx, nz, ng, inputs, norm_gain, united_weight.T, adapter_down, query_up,
+        value_up.transpose(0, 2, 1), request, table_row[:, None],
+    )
 
 
 def local(
@@ -609,23 +662,9 @@
         inputs, norm_gain, united_weight, adapter_down, query_up, value_up, adapter_slot, row_adapter
     )
     lengths = lax.dynamic_slice_in_dim(cache_length, t * rows_here, rows_here, 0)
-    query = got[:, :48].reshape(nt, 2, steps, rows_here, HEAD_DIM)
-    query = query.transpose(2, 3, 0, 1, 4).reshape(steps, rows_here, HEADS, HEAD_DIM)
-    fresh = got[:, 48:].reshape(nt, 2, rows_here, 2, 64).transpose(0, 2, 1, 3, 4)
-    fresh = fresh.reshape(nt, rows_here, 4, 64)[:, :, :steps].transpose(2, 1, 0, 3)
-    key = fresh[..., :32].reshape(steps, rows_here, KV_HEADS, HEAD_DIM)
-    value = fresh[..., 32:].reshape(steps, rows_here, KV_HEADS, HEAD_DIM)
     positions = lengths[None, :] + jnp.arange(steps, dtype=jnp.int32)[:, None]
-    query = rotate(query, positions)
-    key = rotate(key, positions)
-    q = query.reshape(steps, rows_here, KV_HEADS, HEADS // KV_HEADS, HEAD_DIM)
-    q = q.transpose(1, 2, 0, 3, 4).reshape(rows_here, KV_HEADS, 24, HEAD_DIM)
-    q = jnp.pad(q, ((0, 0), (0, 0), (0, 8), (0, 0)))
-    fk = jnp.pad(key.transpose(1, 2, 0, 3), ((0, 0), (0, 0), (0, 13), (0, 0)))
-    fv = jnp.pad(value.transpose(1, 2, 0, 3), ((0, 0), (0, 0), (0, 13), (0, 0)))
-    context = attend(lengths, q, fk, fv, history)
-    context = context[:, :, :24].reshape(rows_here, KV_HEADS, steps, HEADS // KV_HEADS, HEAD_DIM)
-    return context.transpose(2, 0, 1, 3, 4).reshape(steps, rows_here, width)
+    cos, sin = rope_tables(positions.reshape(-1))
+    return attend(lengths, got, cos, sin, history)
 
 
 def solution(mesh):

time: 152 us -> 129 us (0.85)
  local copies, waits for them, and re-layouts: 12.2 us -> 2.26 us
  Pallas kernels: 131 us -> 123 us
  other arithmetic: 7.68 us -> 3.07 us
    pallas_call x1, Pallas kernels: 121 us -> 116 us  [project(): pl.pallas_call(functools.partial(project_kernel, nx, nz, ng, own), out_sh...]
    pad x5 -> x0, local copies, waits for them, and re-layouts: 3.92 us -> none  [the longest x1 0.94 us: projected(): vpad = jnp.pad(value_up, ((0, 0), (0, 0), (32, 64)))]
    convert_element_type x4 -> x1, other arithmetic: 2.68 us -> 0.01 us  [rope_tables(): angles = positions.astype(F32)[:, None] * inverse[None, :]]
    pallas_call x1, Pallas kernels: 9.94 us -> 7.52 us  [attend(): pl.pallas_call(attend_kernel, out_shape=jax.ShapeDtypeStruct((steps, rows...]
    transpose x3 -> x0, local copies, waits for them, and re-layouts: 2.06 us -> none  [the longest x2 2.04 us: local(): return context.transpose(2, 0, 1, 3, 4).reshape(steps, rows_here, width)]
where the time goes in v3:
time: 129 us; the launch traced here: 128 us
  Pallas kernels  123 us (95%)
  other arithmetic  3.07 us (2%)
  local copies, waits for them, and re-layouts  2.26 us (2%)
    pallas_call x1, Pallas kernels, project(): pl.pallas_call(functools.partial(project_kernel, nx, nz, ng, own), out_sh...  116 us
    pallas_call x1, Pallas kernels, attend(): pl.pallas_call(attend_kernel, out_shape=jax.ShapeDtypeStruct((steps, rows...  7.52 us

profile of v3, /device:TPU:8, one launch (start us, length us, event | category | flops | bytes accessed | tf_op | source)
XLA Modules:
  0.0 128.4 jit_solution(7311347825358990255)
XLA Ops:
  0.0 0.8 dynamic_slice.3.lengths
  0.8 0.0 copy-start
  0.8 0.8 select_reduce_fusion.1
  1.6 0.1 fusion
  1.7 0.1 reshape.155
  1.8 0.1 and.55
  1.9 0.1 and.61
  2.0 0.1 convert_element_type.33
  2.1 0.1 fusion.5
  2.1 0.2 reduce_window_sum.13
  2.3 0.1 reduce_window_sum.14
  2.4 0.1 select_reduce_fusion
  2.5 0.1 select_reduce_fusion.2
  2.7 0.7 copy.27.req
  3.4 0.1 fusion.3
  3.5 0.7 pad_maximum_fusion
  4.2 0.1 copy.26
  4.3 0.1 copy.19
  4.5 0.1 copy.21
  4.6 0.8 fusion.1.spot_of_row
  5.4 115.5 %project.1.got = bf16[32,64,128]{2,1,0:T(8,128)(2,1)} custom-call(bf16[3,8,8192]{2,1,0:T(8,128)(2,1)} %inputs.1, bf16[8192]{0:T(1024)(128)(2,1)} %gain.1, bf16[320,8192]{1,0:T(8,128)(2,1)} %bitcast.5, bf16[24,256,128]{2,1,0:T(8,128)(2,1)} %down.1, bf16[24,64,256]{2,1,0:T(8,128)(2,1)} %qup.1, bf16[24,32,64]{2,1,0:T(8,128)(2,1)} %bitcast.6, s32[8,2]{1,0:T(8,128)} %copy.27.req, ...), custom_call_target="tpu_custom_call" | custom-call | tf_op jit(solution)/shard_map/project/pallas_call | solution.py:449
  120.9 0.0 copy-done
  120.9 7.5 %attend.1 = bf16[3,8,8192]{2,1,0:T(8,128)(2,1)} custom-call(s32[8]{0:T(128)} %copy-done, bf16[32,64,128]{2,1,0:T(8,128)(2,1)} %project.1.got, f32[24,128]{1,0:T(8,128)} %get-tuple-element.12.cos, f32[24,128]{1,0:T(8,128)} %get-tuple-element.13.sin, bf16[8,256,2048]{2,1,0:T(8,128)(2,1)} %values.1, bf16[8,256,2048]{2,1,0:T(8,128)(2,1)} %values.1), custom_call_target="tpu_custom_call" | custom-call | tf_op jit(solution)/shard_map/attend/pallas_call | solution.py:595
  (7 shorter events, 0.0 us)
Async XLA Ops:
  0.8 120.1 %copy-start = (s32[8]{0:T(128)}, s32[8]{0:T(128)S(1)}, u32[]{:S(2)}) copy-start(s32[8]{0:T(128)S(1)} %dynamic_slice.3.lengths) | copy-start | bytes 100

commit v4 on v3

--- a/solution.py
+++ b/solution.py
@@ -1,5 +1,6 @@
 import functools
 import heapq
+import math
 
 import jax
 import jax.numpy as jnp
@@ -23,54 +24,73 @@
 MESH = pl.DeviceIdType.MESH
 
 
-def rope_tables(positions):
-    halfway = HEAD_DIM // 2
-    ladder = jnp.arange(halfway).astype(F32) * (2.0 / HEAD_DIM)
-    inverse = jnp.power(F32(rope_base), -ladder)
-    angles = positions.astype(F32)[:, None] * inverse[None, :]
-    cosine = jnp.cos(angles)
-    sine = jnp.sin(angles)
-    return jnp.concatenate([cosine, cosine], axis=-1), jnp.concatenate([-sine, sine], axis=-1)
-
-
-CHORES = (3.0, 16.0, 32.0, 46.0, 56.0, 66.0, 75.0)
+CHORES = (3.0, 16.0, 30.0, 41.0, 50.0, 58.0, 66.0)
 BUSY = {"x": 4.0, "z": 8.0}
-RATE = 45e3
+RATE = 39e3
+LOOK = 6.0
+RANKED = False
 
 
 def ring_order(nx, nz, la, lb):
     sizes = {"A": la * 96 / RATE, "B": lb * 96 / RATE}
     span = {"x": nx, "z": nz}
-    free = {(axis, step): BUSY[axis] for axis in "xz" for step in (1, -1)}
+    links = [("x", 1), ("x", -1), ("z", 1), ("z", -1)]
+    free = {key: BUSY[key[0]] for key in links}
+    waiting = {key: [] for key in links}
+    asleep = {key: True for key in links}
     heap = []
     halves = {}
     out = []
     count = [0]
 
-    def send(now, name, dx, dz, half, axis, step):
+    def push(when, what):
+        count[0] += 1
+        heapq.heappush(heap, (when, count[0], what))
+
+    def send(now, name, dx, dz, half, axis, step, rank):
         key = (axis, step)
-        start = max(free[key], now)
-        free[key] = start + sizes[name] * (1.0 if half is None else 0.5)
-        out.append(("send", key, name, dx % nx, dz % nz, half))
-        ndx = (dx - (step if axis == "x" else 0)) % nx
-        ndz = (dz - (step if axis == "z" else 0)) % nz
         count[0] += 1
-        heapq.heappush(heap, (free[key] + 1.5, count[0], name, ndx, ndz, half, axis, step))
+        heapq.heappush(waiting[key], (rank, count[0], name, dx % nx, dz % nz, half))
+        if asleep[key]:
+            asleep[key] = False
+            push(max(now, free[key] - LOOK), ("pick", key))
+
+    def rank_of(name, axis, hop):
+        if name == "B" and axis == "z":
+            return 0
+        if name == "A" and axis == "x":
+            return 0
+        return 5 - hop if RANKED else 1
 
     def launch(now, name, dx, dz, axis):
         if span[axis] > 2:
-            send(now, name, dx, dz, None, axis, 1)
-            send(now, name, dx, dz, None, axis, -1)
+            for step in (1, -1):
+                send(now, name, dx, dz, None, axis, step, rank_of(name, axis, 0))
         elif span[axis] == 2:
-            send(now, name, dx, dz, 0, axis, 1)
-            send(now, name, dx, dz, 1, axis, -1)
+            send(now, name, dx, dz, 0, axis, 1, rank_of(name, axis, 0))
+            send(now, name, dx, dz, 1, axis, -1, rank_of(name, axis, 0))
 
     launch(0.0, "A", 0, 0, "x")
     launch(0.0, "B", 0, 0, "z")
     launch(0.0, "B", 0, 0, "x")
     launch(0.0, "A", 0, 0, "z")
     while heap:
-        now, _, name, dx, dz, half, axis, step = heapq.heappop(heap)
+        now, _, what = heapq.heappop(heap)
+        if what[0] == "pick":
+            key = what[1]
+            if not waiting[key]:
+                asleep[key] = True
+                continue
+            _, _, name, dx, dz, half = heapq.heappop(waiting[key])
+            axis, step = key
+            free[key] = max(free[key], now) + sizes[name] * (1.0 if half is None else 0.5)
+            out.append(("send", key, name, dx, dz, half))
+            ndx = (dx - (step if axis == "x" else 0)) % nx
+            ndz = (dz - (step if axis == "z" else 0)) % nz
+            push(free[key] + 1.5, ("land", name, ndx, ndz, half, axis, step))
+            push(max(now, free[key] - LOOK), ("pick", key))
+            continue
+        _, name, dx, dz, half, axis, step = what
         tie = (name, dx, dz)
         seen = halves.get(tie, 0)
         halves[tie] = seen + 1
@@ -80,9 +100,9 @@
         far = (-step * (dx if axis == "x" else dz)) % size
         if half is None:
             if far + 1 < size // 2:
-                send(now, name, dx, dz, None, axis, step)
+                send(now, name, dx, dz, None, axis, step, rank_of(name, axis, far))
             elif far + 1 == size // 2:
-                send(now, name, dx, dz, 0 if step > 0 else 1, axis, step)
+                send(now, name, dx, dz, 0 if step > 0 else 1, axis, step, rank_of(name, axis, far))
         if last:
             if name == "A" and axis == "x":
                 launch(now, name, dx, dz, "z")
@@ -93,10 +113,10 @@
 
 def project_kernel(
     nx, nz, ng, own,
-    inputs, gain, w, down, qup, vup, req, spot_of_row,
+    inputs, gain, w, down, qup, vup, spots_and_slots,
     out,
     X, xl, tr, wv, vraw, lbuf, xs, down_o, q_o, v_o, down_f, q_f, v_f, sd, sq, sv, rbuf, rsend, rs,
-    part, pbuf, S, half_sum, sbuf, lrz, lrall, LRq, LRv, Dq, Dv, acc, plain, ob,
+    part, pbuf, S, half_sum, sbuf, lrz, lrall, LRq, LRv, Dq, Dv, plain, ob,
     ssem, gsem, lsem, dsem, fsem, qsem, p1, p2, p3, p4, osem, wsem,
 ):
     nt = nx * nz
@@ -173,9 +193,8 @@
         pieces = [normed[step, :, p * 256 + h * 128 : p * 256 + h * 128 + 128] for h in range(2) for step in range(3)]
         xl[p * 48 : p * 48 + 48, :] = jnp.concatenate(pieces, axis=0).astype(BF16)
     lbuf[pl.ds(mine, 48), :] = xl[pl.ds(mine, 48), :]
-    rsend[...] = jnp.zeros((8, 128), jnp.int32)
-    rsend[0:ng, 0:PAIR_MOST] = req[...]
-    spots = jnp.broadcast_to(spot_of_row[...], (nt * 8, 128)).reshape(nt, 1, 8, 128)
+    rsend[...] = jnp.broadcast_to(spots_and_slots[nt * 8 : nt * 8 + 16, :], (16, 128))
+    spots = jnp.broadcast_to(spots_and_slots[0 : nt * 8, :], (nt * 8, 128)).reshape(nt, 1, 8, 128)
     tr[...] = jnp.broadcast_to(spots, (nt, 3, 8, 128)).reshape(nt * 24, 128)
 
     pl.semaphore_wait(barrier, nt - 1 + ng - 1)
@@ -231,7 +250,7 @@
             down_copy.start()
             down_copy.wait()
             for j in range(PAIR_MOST):
-                slot = rs[k, g, j]
+                slot = rs[k, PAIR_MOST * g + j, 0]
                 sd[k, j] = down_o[slot]
                 sq[k, j] = q_o[slot]
                 sv[k, j] = v_o[slot]
@@ -344,27 +363,33 @@
         lax.fori_loop(0, own // 4, grow(own_table(q_o), own_table(v_o), 0), 0)
         lax.fori_loop(0, ng * PAIR_MOST // 4, grow(far_table(q_f), far_table(v_f), own), 0)
 
-    kt = 512
-
-    def base_of(dz):
+    kt = 128 * math.gcd(ta, tiles, 4)
+    seen = {dz: [] for dz in range(nz)}
+
+    def multiply(dz, name):
         rows = pl.ds(pl.multiple_of(lax.rem(z + dz % nz, nz) * (nx * 48), 16), nx * 48)
-        acc[...] = jnp.zeros(acc.shape, F32)
+        lo, n = whole[name]
 
         def body(k, carry):
-            cols = pl.ds(pl.multiple_of(k * kt, kt), kt)
+            cols = pl.ds(pl.multiple_of(lo + k * kt, kt), kt)
             for h in range(2):
-                acc[h] += lax.dot_general(
-                    X[rows, cols], wv[h, :, cols], (((1,), (1,)), ((), ())), preferred_element_type=F32
+                plain[dz, h] += lax.dot_general(
+                    wv[h, :, cols], X[rows, cols], (((1,), (1,)), ((), ())), preferred_element_type=F32
                 )
             return carry
 
-        lax.fori_loop(0, K2 // kt, body, 0)
-        first = acc[0].reshape(nx * 3, 2, 8, NW)[:, 0]
-        second = acc[1].reshape(nx * 3, 2, 8, NW)[:, 1]
-        plain[dz % nz] = (first + second).reshape(nx * 24, NW)
+        if name not in seen[dz] and not seen[dz]:
+            plain[dz] = jnp.zeros(plain.shape[1:], F32)
+        seen[dz].append(name)
+        lax.fori_loop(0, n // kt, body, 0)
+
+    def base_of(dz):
+        first = plain[dz, 0].T.reshape(nx * 3, 2, 8, NW)[:, 0]
+        second = plain[dz, 1].T.reshape(nx * 3, 2, 8, NW)[:, 1]
+        return (first + second).reshape(nx * 24, NW)
 
     def finish(dz):
-        base = plain[dz % nz]
+        base = base_of(dz % nz)
         zz = lax.rem(z + dz % nz, nz)
         rows = pl.ds(pl.multiple_of(zz * (nx * 24), 8), nx * 24)
         query = base[:, :256] + adapter_scale * Dq[rows, :]
@@ -397,8 +422,7 @@
     loaded = []
     ready = []
     based = []
-    missing = {dz: 2 * nx for dz in range(nz)}
-    missing[0] -= 2
+    missing = {(dz, name): nx - (dz == 0) for dz in range(nz) for name in "AB"}
 
     def settle(now):
         while chores and chores[0][0] <= now:
@@ -408,9 +432,10 @@
                 for load in loads[3:5]:
                     load.wait()
                 loaded.append(1)
-            dz = ready.pop(0)
-            base_of(dz)
-            based.append(dz)
+            dz, name = ready.pop(0)
+            multiply(dz, name)
+            if len(seen[dz]) == 2:
+                based.append(dz)
         while based and not chores:
             finish(based.pop(0))
 
@@ -423,9 +448,9 @@
             piece_half, last = (None, True) if half is None else half
             expect(name, dx, dz, piece_half)
             if last:
-                missing[dz] -= 1
-                if missing[dz] == 0:
-                    ready.append(dz)
+                missing[dz, name] -= 1
+                if missing[dz, name] == 0:
+                    ready.append((dz, name))
     settle(1e9)
 
     for dz in range(nz):
@@ -436,7 +461,7 @@
         copy.wait_send()
 
 
-def project(nx, nz, ng, inputs, gain, w, down, qup, vup, req, spot_of_row):
+def project(nx, nz, ng, inputs, gain, w, down, qup, vup, spots_and_slots):
     nt = nx * nz
     K2 = inputs.shape[2] // 2
     own = down.shape[0]
@@ -449,7 +474,7 @@
     return pl.pallas_call(
         functools.partial(project_kernel, nx, nz, ng, own),
         out_shape=jax.ShapeDtypeStruct((nt, 64, 128), BF16),
-        in_specs=[vmem, vmem, hbm, hbm, hbm, hbm, vmem, vmem],
+        in_specs=[vmem, vmem, hbm, hbm, hbm, hbm, vmem],
         out_specs=vmem,
         scratch_shapes=[
             pltpu.VMEM((nt * 48, K2), BF16),
@@ -468,9 +493,9 @@
             pltpu.VMEM((ng, 2) + down.shape[1:], BF16),
             pltpu.VMEM((ng, 2, 64, 256), BF16),
             pltpu.VMEM((ng, 2, 64, 128), BF16),
-            pltpu.VMEM((ng, 8, 128), jnp.int32),
-            pltpu.VMEM((8, 128), jnp.int32),
-            pltpu.SMEM((ng, 8, 128), jnp.int32),
+            pltpu.VMEM((ng, 16, 128), jnp.int32),
+            pltpu.VMEM((16, 128), jnp.int32),
+            pltpu.SMEM((ng, 16, 128), jnp.int32),
             pltpu.VMEM((rows, 128), F32),
             pltpu.VMEM((nx, nz * 24, 128), BF16),
             pltpu.VMEM((nx, nz * 24, 128), BF16),
@@ -482,8 +507,7 @@
             pltpu.VMEM((rows, 128), F32),
             pltpu.VMEM((rows, 256), F32),
             pltpu.VMEM((rows, 128), F32),
-            pltpu.VMEM((2, nx * 48, NW), F32),
-            pltpu.VMEM((nz, nx * 24, NW), F32),
+            pltpu.VMEM((nz, 2, NW, nx * 48), F32),
             pltpu.VMEM((nz, nx, 64, 128), BF16),
             DMA((sends,)),
             DMA((2, nx, nz, 2)),
@@ -502,11 +526,29 @@
             collective_id=0, has_side_effects=True, vmem_limit_bytes=56 * MIB
         ),
         name="project",
-    )(inputs, gain, w, down, qup, vup, req, spot_of_row)
-
-
-def attend_kernel(lengths, got, cos, sin, keys, values, out, scr, res):
+    )(inputs, gain, w, down, qup, vup, spots_and_slots)
+
+
+def attend_kernel(all_lengths, got, keys, values, out, scr, res, cos, sin):
     rows_here, window, _ = keys.shape
+    first_row = lax.axis_index("tensor") * rows_here
+    lengths = [all_lengths[first_row + r] for r in range(rows_here)]
+
+    @pl.when(pl.program_id(0) == 0)
+    def _():
+        sublane = lax.broadcasted_iota(jnp.int32, (8, 128), 0)
+        column = lax.broadcasted_iota(jnp.int32, (8, 128), 1)
+        ladder = lax.rem(column, 64).astype(F32) * (2.0 / HEAD_DIM)
+        inverse = jnp.power(F32(rope_base), -ladder)
+        position = jnp.zeros((8, 128), jnp.int32)
+        for r in range(rows_here):
+            position = jnp.where(sublane == r, lengths[r], position)
+        for k in range(3):
+            angles = (position + k).astype(F32) * inverse
+            cos[8 * k : 8 * k + 8, :] = jnp.cos(angles)
+            sine = jnp.sin(angles)
+            sin[8 * k : 8 * k + 8, :] = jnp.where(column < 64, -sine, sine)
+
     factor = HEAD_DIM ** (-0.5)
     dims = (((1,), (1,)), ((), ()))
     lane = lax.broadcasted_iota(jnp.int32, (8, 128), 1) // 32
@@ -588,9 +630,9 @@
                 out[k, :, spot] = res[b, pl.ds(hh * 3 + k, 8, stride=8), :].astype(BF16)
 
 
-def attend(lengths, got, cos, sin, hist):
+def attend(all_lengths, got, hist):
     rows, window, width = hist.shape
-    steps = cos.shape[0] // rows
+    steps = 3
     pairs = got.shape[0] // 8
     return pl.pallas_call(
         attend_kernel,
@@ -599,16 +641,19 @@
         in_specs=[
             pl.BlockSpec(memory_space=pltpu.SMEM),
             pl.BlockSpec((8, 64, 128), lambda h: (h, 0, 0)),
-            pl.BlockSpec((steps * rows, 128), lambda h: (0, 0)),
-            pl.BlockSpec((steps * rows, 128), lambda h: (0, 0)),
             pl.BlockSpec((rows, window, 2 * HEAD_DIM), lambda h: (0, 0, h)),
             pl.BlockSpec((rows, window, 2 * HEAD_DIM), lambda h: (0, 0, KV_HEADS // 2 + h)),
         ],
         out_specs=pl.BlockSpec((steps, rows, 2 * HEADS // KV_HEADS * HEAD_DIM), lambda h: (0, 0, h)),
-        scratch_shapes=[pltpu.VMEM((8, 64, 128), F32), pltpu.VMEM((8, 64, 128), F32)],
+        scratch_shapes=[
+            pltpu.VMEM((8, 64, 128), F32),
+            pltpu.VMEM((8, 64, 128), F32),
+            pltpu.VMEM((steps * rows, 128), F32),
+            pltpu.VMEM((steps * rows, 128), F32),
+        ],
         compiler_params=pltpu.CompilerParams(vmem_limit_bytes=56 * MIB),
         name="attend",
-    )(lengths, got, cos, sin, hist, hist)
+    )(all_lengths, got, hist, hist)
 
 
 def routing(adapter_slot, row_adapter, store, groups, home):
@@ -645,9 +690,11 @@
     nz = nt // nx
     g = lax.axis_index("group")
     request, table_row = routing(adapter_slot, row_adapter, adapter_down.shape[0], ng, g)
+    asked = jnp.pad(request.reshape(-1), (0, 16 - ng * PAIR_MOST))
+    spots_and_slots = jnp.concatenate([table_row, asked])
     return project(
         nx, nz, ng, inputs, norm_gain, united_weight.T, adapter_down, query_up,
-        value_up.transpose(0, 2, 1), request, table_row[:, None],
+        value_up.transpose(0, 2, 1), spots_and_slots[:, None],
     )
 
 
@@ -655,16 +702,10 @@
     inputs, norm_gain, united_weight, adapter_down, query_up, value_up, history,
     adapter_slot, row_adapter, cache_length,
 ):
-    steps, rows_here, width = inputs.shape
-    nt = lax.axis_size("tensor")
-    t = lax.axis_index("tensor")
     got = projected(
         inputs, norm_gain, united_weight, adapter_down, query_up, value_up, adapter_slot, row_adapter
     )
-    lengths = lax.dynamic_slice_in_dim(cache_length, t * rows_here, rows_here, 0)
-    positions = lengths[None, :] + jnp.arange(steps, dtype=jnp.int32)[:, None]
-    cos, sin = rope_tables(positions.reshape(-1))
-    return attend(lengths, got, cos, sin, history)
+    return attend(cache_length, got, history)
 
 
 def solution(mesh):

time: 129 us -> 123 us (0.953)
  Pallas kernels: 123 us -> 119 us
  other arithmetic: 3.07 us -> 1.49 us
    pallas_call x1, Pallas kernels: 116 us -> 112 us  [project(): pl.pallas_call(functools.partial(project_kernel, nx, nz, ng, own), out_sh...]
where the time goes in v4:
time: 123 us; the launch traced here: 122 us
  Pallas kernels  119 us (97%)
  other arithmetic  1.49 us (1%)
  local copies, waits for them, and re-layouts  1.27 us (1%)
    pallas_call x1, Pallas kernels, project(): pl.pallas_call(functools.partial(project_kernel, nx, nz, ng, own), out_sh...  112 us
    pallas_call x1, Pallas kernels, attend(): pl.pallas_call(attend_kernel, out_shape=jax.ShapeDtypeStruct((steps, rows...  7.45 us

profile of v4, /device:TPU:8, one launch (start us, length us, event | category | flops | bytes accessed | tf_op | source)
XLA Modules:
  0.0 122.0 jit_solution(13956691403423616419)
XLA Ops:
  0.0 0.8 select_reduce_fusion.1
  0.8 0.1 fusion
  0.9 0.1 reshape.69
  1.0 0.1 and.42
  1.1 0.1 and.44
  1.2 0.1 fusion.3
  1.3 0.2 reduce_window_sum.13
  1.4 0.1 reduce_window_sum.14
  1.5 0.1 select_reduce_fusion
  1.7 0.1 select_reduce_fusion.2
  1.8 0.1 copy.12
  1.9 0.1 reshape.70
  2.0 0.8 broadcast_in_dim.49.spots_and_slots
  2.8 111.8 %project.1.got = bf16[32,64,128]{2,1,0:T(8,128)(2,1)} custom-call(bf16[3,8,8192]{2,1,0:T(8,128)(2,1)} %inputs.1, bf16[8192]{0:T(1024)(128)(2,1)} %gain.1, bf16[320,8192]{1,0:T(8,128)(2,1)} %bitcast.2, bf16[24,256,128]{2,1,0:T(8,128)(2,1)} %down.1, bf16[24,64,256]{2,1,0:T(8,128)(2,1)} %qup.1, bf16[24,32,64]{2,1,0:T(8,128)(2,1)} %bitcast.3, ...), custom_call_target="tpu_custom_call" | custom-call | tf_op jit(solution)/shard_map/project/pallas_call | solution.py:474
  114.6 7.5 %attend.1 = bf16[3,8,8192]{2,1,0:T(8,128)(2,1)} custom-call(s32[256]{0:T(256)} %all_lengths.1, bf16[32,64,128]{2,1,0:T(8,128)(2,1)} %project.1.got, bf16[8,256,2048]{2,1,0:T(8,128)(2,1)} %values.1, bf16[8,256,2048]{2,1,0:T(8,128)(2,1)} %values.1), custom_call_target="tpu_custom_call" | custom-call | tf_op jit(solution)/shard_map/attend/pallas_call | solution.py:637
  (5 shorter events, 0.0 us)

commit v5 on v4

--- a/solution.py
+++ b/solution.py
@@ -24,7 +24,7 @@
 MESH = pl.DeviceIdType.MESH
 
 
-CHORES = (3.0, 16.0, 30.0, 41.0, 50.0, 58.0, 66.0)
+CHORES = (3.0, 14.0, 28.0, 40.0, 50.0, 58.0, 66.0)
 BUSY = {"x": 4.0, "z": 8.0}
 RATE = 39e3
 LOOK = 6.0

time: 123 us -> 126 us (1.024); the launches traced: 122 us -> 126 us
  Pallas kernels: 119 us -> 123 us
    pallas_call x1, Pallas kernels: 112 us -> 116 us  [project(): pl.pallas_call(functools.partial(project_kernel, nx, nz, ng, own), out_sh...]
where the time goes in v5:
time: 126 us
  Pallas kernels  123 us (98%)
  other arithmetic  1.49 us (1%)
  local copies, waits for them, and re-layouts  1.27 us (1%)
    pallas_call x1, Pallas kernels, project(): pl.pallas_call(functools.partial(project_kernel, nx, nz, ng, own), out_sh...  116 us
    pallas_call x1, Pallas kernels, attend(): pl.pallas_call(attend_kernel, out_shape=jax.ShapeDtypeStruct((steps, rows...  7.45 us

profile of v5, /device:TPU:8, one launch (start us, length us, event | category | flops | bytes accessed | tf_op | source)
XLA Modules:
  0.0 126.3 jit_solution(13993675670532385566)
XLA Ops:
  0.0 0.8 select_reduce_fusion.1
  0.8 0.1 fusion
  0.9 0.1 reshape.69
  1.0 0.1 and.42
  1.1 0.1 and.44
  1.2 0.1 fusion.3
  1.3 0.2 reduce_window_sum.13
  1.4 0.1 reduce_window_sum.14
  1.5 0.1 select_reduce_fusion
  1.7 0.1 select_reduce_fusion.2
  1.8 0.1 copy.12
  1.9 0.1 reshape.70
  2.0 0.8 broadcast_in_dim.49.spots_and_slots
  2.8 116.0 %project.1.got = bf16[32,64,128]{2,1,0:T(8,128)(2,1)} custom-call(bf16[3,8,8192]{2,1,0:T(8,128)(2,1)} %inputs.1, bf16[8192]{0:T(1024)(128)(2,1)} %gain.1, bf16[320,8192]{1,0:T(8,128)(2,1)} %bitcast.2, bf16[24,256,128]{2,1,0:T(8,128)(2,1)} %down.1, bf16[24,64,256]{2,1,0:T(8,128)(2,1)} %qup.1, bf16[24,32,64]{2,1,0:T(8,128)(2,1)} %bitcast.3, ...), custom_call_target="tpu_custom_call" | custom-call | tf_op jit(solution)/shard_map/project/pallas_call | solution.py:474
  118.8 7.5 %attend.1 = bf16[3,8,8192]{2,1,0:T(8,128)(2,1)} custom-call(s32[256]{0:T(256)} %all_lengths.1, bf16[32,64,128]{2,1,0:T(8,128)(2,1)} %project.1.got, bf16[8,256,2048]{2,1,0:T(8,128)(2,1)} %values.1, bf16[8,256,2048]{2,1,0:T(8,128)(2,1)} %values.1), custom_call_target="tpu_custom_call" | custom-call | tf_op jit(solution)/shard_map/attend/pallas_call | solution.py:637
  (5 shorter events, 0.0 us)
